TPU v7x, 1024 devices: a whole 4x8x16 slice. The times are simulated.
1024 devices in a mesh: replica: 16 (over y, core), owner: 64 (over z, x).
Axes of the slice: x: 4, y: 8, z: 16, core: 2. Of those that a mesh axis runs over, the one named last changes fastest.
Arguments:
- grad_parts: bfloat16 [16, 144, 512, 512], P('replica', None, 'owner'), may hold values from -0.29882812 to 0.29882812
- owner_of: int32 [144, 1], replicated, may hold values from 0 to 63; in each aligned block of 144 rows (0 to 143, 144 to 287, ...) at most 5 rows name the same one
- stats_left: bfloat16 [64, 5, 512, 512], P('owner', None, 'replica'), may hold values from -6 to 6
- stats_right: bfloat16 [64, 5, 512, 512], P('owner', None, 'replica'), may hold values from -6 to 6
- basis_left: bfloat16 [64, 5, 512, 512], P('owner'), may hold values from -0.25 to 0.25
- basis_right: bfloat16 [64, 5, 512, 512], P('owner'), may hold values from -0.25 to 0.25
- moment_first: float32 [64, 5, 512, 512], P('owner', None, 'replica'), may hold values from -0.6 to 0.6
- moment_second: float32 [64, 5, 512, 512], P('owner', None, 'replica'), may hold values from 0.01 to 0.04
Outputs:
- new_left: bfloat16 [64, 5, 512, 512], P('owner', None, 'replica')
- new_right: bfloat16 [64, 5, 512, 512], P('owner', None, 'replica')
- new_first: float32 [64, 5, 512, 512], P('owner', None, 'replica')
- new_second: float32 [64, 5, 512, 512], P('owner', None, 'replica')
- update: bfloat16 [144, 512, 512], P(None, 'owner', 'replica')
Inputs may be any that keep to these rules, and one draw needn't show every extreme that they name: owner_of[b, 0] is the owner of block b; every owner is named, none by more than 5 blocks, and one by exactly 5.
All inputs are finite; a program needn't handle non-finite values.
Results may differ from a plain program's by a relative error of at most 0.02.
Values may be sent and summed in bfloat16 or wider, within the bound.
A program may use at most 32 MiB of HBM per device.

v0:
```python
import jax
import jax.numpy as jnp
from jax import lax
from jax.sharding import PartitionSpec as P

BETA_FIRST = 0.9
BETA_SECOND = 0.95
EPSILON = 1e-08


def slot_selector(owner_of, owners_count, slot_count):
    owners = owner_of[:, 0]
    onehot = (owners[:, None] == jnp.arange(owners_count, dtype=jnp.int32)[None, :]).astype(
        jnp.int32
    )
    before = jnp.cumsum(onehot, axis=0) - onehot
    slot_rank = jnp.sum(before * onehot, axis=1)
    flat_slot = slot_rank * owners_count + owners
    places = jnp.arange(slot_count * owners_count, dtype=jnp.int32)
    return (places[:, None] == flat_slot[None, :]).astype(jnp.bfloat16)


def shards(
    grad_parts,
    owner_of,
    stats_left,
    stats_right,
    basis_left,
    basis_right,
    moment_first,
    moment_second,
):
    owners_count = lax.axis_size("owner")
    team_size = lax.axis_size("replica")
    slot_count = stats_left.shape[1]
    block_width = stats_left.shape[3]
    slab_width = block_width // team_size
    row_width = block_width // owners_count
    first_row = lax.axis_index("replica") * slab_width
    summed = lax.psum_scatter(
        grad_parts[0].astype(jnp.float32).astype(jnp.bfloat16),
        "replica",
        scatter_dimension=2,
        tiled=True,
    ).astype(jnp.float32)
    blocks = summed.shape[0]
    grad_rows = summed.astype(jnp.bfloat16).reshape(blocks, row_width * slab_width)
    selector = slot_selector(owner_of, owners_count, slot_count)
    outgoing = jnp.dot(selector, grad_rows, preferred_element_type=jnp.float32).astype(jnp.bfloat16)
    outgoing = outgoing.reshape(slot_count, owners_count, row_width * slab_width)
    arrived = lax.all_to_all(outgoing, "owner", split_axis=1, concat_axis=1, tiled=True)
    own_columns = arrived.reshape(slot_count, block_width, slab_width)
    left_basis = basis_left[0]
    right_basis = basis_right[0]
    left_cols = lax.dynamic_slice_in_dim(left_basis, first_row, slab_width, 2)
    right_rows = lax.dynamic_slice_in_dim(right_basis, first_row, slab_width, 1)
    gathered = lax.all_gather(own_columns, "replica", axis=2, tiled=True)
    mine_rows = lax.dynamic_slice_in_dim(gathered, first_row, slab_width, 1)
    left_term = jnp.einsum("sic,sjc->sij", mine_rows, gathered, preferred_element_type=jnp.float32)
    right_term = jnp.einsum(
        "sai,saj->sij", own_columns, gathered, preferred_element_type=jnp.float32
    )
    half_term = jnp.einsum("sai,saj->sij", left_cols, gathered, preferred_element_type=jnp.float32)
    new_left = (
        BETA_SECOND * stats_left[0].astype(jnp.float32) + (1.0 - BETA_SECOND) * left_term
    ).astype(jnp.bfloat16)
    new_right = (
        BETA_SECOND * stats_right[0].astype(jnp.float32) + (1.0 - BETA_SECOND) * right_term
    ).astype(jnp.bfloat16)
    half_rot = half_term.astype(jnp.bfloat16)
    rotated = jnp.einsum("sic,scj->sij", half_rot, right_basis, preferred_element_type=jnp.float32)
    new_first = BETA_FIRST * moment_first[0] + (1.0 - BETA_FIRST) * rotated
    new_second = BETA_SECOND * moment_second[0] + (1.0 - BETA_SECOND) * rotated * rotated
    direction = (new_first / (jnp.sqrt(new_second) + EPSILON)).astype(jnp.bfloat16)
    all_rows = lax.all_gather(direction, "replica", axis=1, tiled=True)
    back_term = jnp.einsum("sic,sjc->sij", all_rows, right_rows, preferred_element_type=jnp.float32)
    back_half = back_term.astype(jnp.bfloat16)
    update_cols = jnp.einsum(
        "sia,saj->sij", left_basis, back_half, preferred_element_type=jnp.float32
    ).astype(jnp.bfloat16)
    leaving = update_cols.reshape(slot_count, owners_count, row_width * slab_width)
    returned = lax.all_to_all(leaving, "owner", split_axis=1, concat_axis=1, tiled=True)
    picked = jnp.dot(
        selector.T,
        returned.reshape(slot_count * owners_count, row_width * slab_width),
        preferred_element_type=jnp.float32,
    ).astype(jnp.bfloat16)
    update = picked.reshape(blocks, row_width, slab_width)
    return (new_left[None], new_right[None], new_first[None], new_second[None], update)


def solution(mesh):
    return jax.shard_map(
        shards,
        mesh=mesh,
        in_specs=(
            P("replica", None, "owner", None),
            P(),
            P("owner", None, "replica", None),
            P("owner", None, "replica", None),
            P("owner", None, None, None),
            P("owner", None, None, None),
            P("owner", None, "replica", None),
            P("owner", None, "replica", None),
        ),
        out_specs=(
            P("owner", None, "replica", None),
            P("owner", None, "replica", None),
            P("owner", None, "replica", None),
            P("owner", None, "replica", None),
            P(None, "owner", "replica"),
        ),
        check_vma=False,
    )
```

profile of v0, /device:TPU:1, one launch (start us, length us, event | category | flops | bytes accessed | tf_op | source)
XLA Modules:
  0.0 268.4 jit_solution(10776928481632325758)
XLA Ops:
  7.2 4.6 %copy.38 = bf16[1,144,8,512]{1,2,3,0:T(8,128)(2,1)} copy(bf16[1,144,8,512]{3,2,1,0:T(8,128)(2,1)} %param.8) | data formatting | bytes 2359296 | tf_op args[0]
  12.0 0.6 reduce-window.6
  12.6 0.2 slice_reduce_fusion
  12.8 0.1 bitcast_bitcast_fusion
  13.0 74.3 %reduce-scatter.2.cloned.1.call-done = bf16[144,8,32]{0,1,2:T(8,128)(2,1)} async-done(((bf16[144,8,512]{0,1,2:T(8,128)(2,1)}), bf16[144,8,32]{0,1,2:T(8,128)(2,1)}) %reduce-scatter.2.cloned.1.call-update) | async-done | bytes 73744 | tf_op jit(solution)/shard_map/reduce_scatter | solution.py:40
  87.3 0.9 copy.39
  88.2 0.2 convolution_convert_fusion.2
  88.5 0.1 copy.40
  88.6 30.9 %all_to_all.10 = bf16[5,64,256]{2,0,1:T(8,128)(2,1)S(1)} all-to-all(bf16[5,64,256]{2,0,1:T(8,128)(2,1)S(1)} %copy.40), channel_id=1, replica_groups=mesh['replica'=16,'owner'=64] {'owner'}, dimensions={1} | all-to-all | bytes 327680 | tf_op jit(solution)/shard_map/all_to_all | solution.py:51
  119.5 0.3 reshape.63
  119.8 0.9 copy.42
  120.7 44.0 %all-gather.3.cloned.1.call-done = bf16[5,512,512]{1,2,0:T(8,128)(2,1)} async-done(((bf16[5,512,32]{1,2,0:T(8,128)(2,1)}), bf16[5,512,512]{1,2,0:T(8,128)(2,1)}) %all-gather.3.cloned.1.call-update) | async-done | bytes 2621456 | tf_op jit(solution)/shard_map/all_gather | solution.py:57
  164.7 4.6 %divide_convert_fusion = (bf16[5,32,512]{2,1,0:T(8,128)(2,1)}, f32[1,5,32,512]{3,2,1,0:T(8,128)}, f32[1,5,32,512]{3,2,1,0:T(8,128)}) fusion(f32[1,5,32,512]{3,2,1,0:T(8,128)} %param.14, f32[1,5,32,512]{3,2,1,0:T(8,128)} %param.15, bf16[1,5,512,512]{3,2,1,0:T(8,128)(2,1)S(1)} %copy-done, bf16[5,512,512]{1,2,0:T(8,128)(2,1)} %all-gather.3.cloned.1.call-done, ...), kind=kOutput, calls=%fused_computation.24 | convolution fusion | flops 168673280 | bytes 7372804 | tf_op jit(solution)/shard_map/sic,scj->sij/dot_general | solution.py:71
  169.4 47.3 %all-gather.5.cloned.1.call-done = bf16[5,512,512]{2,1,0:T(8,128)(2,1)} async-done(((bf16[5,32,512]{2,1,0:T(8,128)(2,1)}), bf16[5,512,512]{2,1,0:T(8,128)(2,1)}) %all-gather.5.cloned.1.call-update) | async-done | bytes 2621456 | tf_op jit(solution)/shard_map/all_gather | solution.py:75
  216.7 4.1 %fusion.11 = bf16[5,512,32]{1,2,0:T(8,128)(2,1)S(1)} fusion(bf16[1,5,512,512]{3,2,1,0:T(8,128)(2,1)} %param.12, bf16[5,512,512]{2,1,0:T(8,128)(2,1)} %all-gather.5.cloned.1.call-done, bf16[1,5,512,512]{3,2,1,0:T(8,128)(2,1)S(1)} %copy-done, s32[]{:T(128)S(6)} %select_n.2), kind=kOutput, calls=%fused_computation.14 | convolution fusion | flops 167936000 | bytes 5570564 | tf_op jit(solution)/shard_map/sia,saj->sij/dot_general | solution.py:78
  220.9 1.1 copy.46
  221.9 1.6 reshape.64
  223.5 0.8 copy.47
  224.3 16.1 %all-to-all-start.1 = ((bf16[5,64,256]{2,0,1:T(8,128)(2,1)}), bf16[5,64,256]{2,0,1:T(8,128)(2,1)S(1)}, u32[]{:S(2)}, u32[]{:S(2)}) async-start(bf16[5,64,256]{2,0,1:T(8,128)(2,1)} %copy.47), calls=%async_computation.2 | async-start | bytes 524288 | tf_op jit(solution)/shard_map/all_to_all | solution.py:82
  240.4 3.5 %fusion.15 = bf16[1,5,32,512]{3,2,1,0:T(8,128)(2,1)} fusion(bf16[5,512,512]{1,2,0:T(8,128)(2,1)} %all-gather.3.cloned.1.call-done, s32[]{:T(128)S(6)} %select_n.2, bf16[1,5,32,512]{3,2,1,0:T(8,128)(2,1)} %param.10), kind=kOutput, calls=%fused_computation.16 | convolution fusion | flops 84295680 | bytes 3604484 | tf_op jit(solution)/shard_map/sic,sjc->sij/dot_general | solution.py:59
  244.0 1.6 fusion.14
  245.5 15.2 %all-to-all-done.1 = bf16[5,64,256]{2,0,1:T(8,128)(2,1)S(1)} async-done(((bf16[5,64,256]{2,0,1:T(8,128)(2,1)}), bf16[5,64,256]{2,0,1:T(8,128)(2,1)S(1)}, u32[]{:S(2)}, u32[]{:S(2)}) %all-to-all-start.1) | async-done | bytes 163872 | tf_op jit(solution)/shard_map/all_to_all | solution.py:82
  260.8 0.3 convolution_convert_fusion.3
  261.1 0.8 copy.49
  (22 shorter events, 0.4 us)
Async XLA Ops:
  7.2 157.5 %copy-start = (bf16[1,5,512,512]{3,2,1,0:T(8,128)(2,1)S(1)}, bf16[1,5,512,512]{3,2,1,0:T(8,128)(2,1)}, u32[]{:S(2)}) copy-start(bf16[1,5,512,512]{3,2,1,0:T(8,128)(2,1)} %param.13) | copy-start | bytes 7864324
  7.2 4.8 %copy-start.3 = (s32[144,1]{0,1:T(1,128)S(1)}, s32[144,1]{0,1:T(1,128)}, u32[]{:S(2)}) copy-start(s32[144,1]{0,1:T(1,128)} %param.9) | copy-start | bytes 1732
  7.2 80.1 %reduce-scatter.2.cloned.1.call-start = ((), (), s32[]{:S(2)}) async-start(), calls=%async_computation.3 | async-start | bytes 2228224 | tf_op jit(solution)/shard_map/reduce_scatter | solution.py:40
  11.9 152.8 %all-gather.3.cloned.1.call-start = ((), (), s32[]{:S(2)}) async-start(), calls=%async_computation.4 | async-start | bytes 2785280 | tf_op jit(solution)/shard_map/all_gather | solution.py:57
  120.7 96.0 %all-gather.5.cloned.1.call-start = ((), (), s32[]{:S(2)}) async-start(), calls=%async_computation.5 | async-start | bytes 2785280 | tf_op jit(solution)/shard_map/all_gather | solution.py:75
  224.3 36.4 %all-to-all-start.1 = ((bf16[5,64,256]{2,0,1:T(8,128)(2,1)}), bf16[5,64,256]{2,0,1:T(8,128)(2,1)S(1)}, u32[]{:S(2)}, u32[]{:S(2)}) async-start(bf16[5,64,256]{2,0,1:T(8,128)(2,1)} %copy.47), calls=%async_computation.2 | async-start | bytes 524288 | tf_op jit(solution)/shard_map/all_to_all | solution.py:82
  240.4 3.5 %copy-start.1 = (bf16[5,512,512]{1,2,0:T(8,128)(2,1)S(1)}, bf16[5,512,512]{1,2,0:T(8,128)(2,1)}, u32[]{:S(2)}) copy-start(bf16[5,512,512]{1,2,0:T(8,128)(2,1)} %all-gather.3.cloned.1.call-done) | copy-start | bytes 7864324
  240.4 3.5 %copy-start.2 = (bf16[1,5,32,512]{3,2,1,0:T(8,128)(2,1)S(1)}, bf16[1,5,32,512]{3,2,1,0:T(8,128)(2,1)}, u32[]{:S(2)}) copy-start(bf16[1,5,32,512]{3,2,1,0:T(8,128)(2,1)} %param.11) | copy-start | bytes 491524
Sparse Core Ops, SparseCore 0:
  12.0 75.2 reduce-scatter.1
  120.8 43.8 all-gather.2
  169.5 47.1 all-gather.4
where the time goes:
time: 270 us; the launch traced here: 268 us
  waiting for transfers between devices  181 us (67%)
  blocking collectives  30.9 us (11%)
  starting transfers between devices  16.2 us (6%)
  matrix products  14.4 us (5%)
  between operations  13.9 us (5%)
  local copies, waits for them, and re-layouts  11.3 us (4%)
    reduce_scatter x1, waiting for transfers between devices, shards(): lax.psum_scatter(grad_parts[0].astype(jnp.float32).astype(jnp.bfloat16),...  74.3 us
    all_gather x1, waiting for transfers between devices, shards(): all_rows = lax.all_gather(direction, 'replica', axis=1, tiled=True)  47.3 us
    all_gather x1, waiting for transfers between devices, shards(): gathered = lax.all_gather(own_columns, 'replica', axis=2, tiled=True)  44 us
    all_to_all x1, blocking collectives, shards(): lax.all_to_all(outgoing, 'owner', split_axis=1, concat_axis=1, tiled=True)  30.9 us
    all_to_all x1, starting transfers between devices, shards(): lax.all_to_all(leaving, 'owner', split_axis=1, concat_axis=1, tiled=True)  16.1 us
    all_to_all x1, waiting for transfers between devices, shards(): lax.all_to_all(leaving, 'owner', split_axis=1, concat_axis=1, tiled=True)  15.2 us
  transfers between devices with their start and end apart: 4, of which 4 were waited for; matrix products, arithmetic and copies ran while one was open for 2% of the time, Pallas kernels for 0%

commit v1 on v0

v1 whole, which is shorter than its diff:
```python
import jax
import jax.numpy as jnp
from jax import lax
from jax.experimental import pallas as pl
from jax.experimental.pallas import tpu as pltpu
from jax.sharding import PartitionSpec as P

BETA_FIRST = 0.9
BETA_SECOND = 0.95
EPSILON = 1e-08
MESH = pl.DeviceIdType.MESH
BF = jnp.bfloat16
F32 = jnp.float32
NY, NX, NZ = 8, 4, 16
NB, PADB = 144, 256
SLOTS = 5
SUBS, SUBROWS = 3, 48
PAIRS = ((0, 1), (2, 3), (4, 4))
PAIR_CORE = (0, 1, 0)


def mm(a, b):
    return jnp.dot(a, b, preferred_element_type=F32)


def mm_t(a, b):
    return lax.dot_general(a, b, (((1,), (1,)), ((), ())), preferred_element_type=F32)


def iota(shape, axis):
    return lax.broadcasted_iota(jnp.int32, shape, axis)


def onehot(a, b):
    return jnp.where(a == b, 1.0, 0.0).astype(BF)


def kernel(
    grad, own_col, own_row, stats_l, stats_r, basis_l, basis_r, mom1, mom2,
    out_l, out_r, out_1, out_2, out_u,
    go, gx, chunk, rs_recv, rs_send, summed, place, v1, w1, xs1, gall,
    ql, qr, qrs, sl, sr, m1, m2, arot, pm, perm2, perm3, ohfin, pick,
    bmsg, bb, ub, w2, xs2, yb,
    s_in, s_core, r_core, s_rs, r_rs, s_cag, r_cag, s_z1, r_z1, s_x1, r_x1,
    s_ag, r_ag, s_sib, r_sib, s_b, r_b, s_z2, r_z2, s_x2, r_x2, s_y, r_y,
):
    rep = lax.axis_index("replica")
    own = lax.axis_index("owner")
    y, c = rep // 2, rep % 2
    z, x = own // NX, own % NX
    sib = (y * 2 + (1 - c), own)
    zhalf = z // 8
    active = c == zhalf

    def at_y(yy, cc):
        return (lax.rem(yy + 2 * NY, NY) * 2 + cc, own)

    def at_z(zz):
        return (rep, zz * NX + x)

    def at_x(xx):
        return (rep, z * NX + xx)

    def remote(src, dst, ssem, rsem, dev):
        return pltpu.make_async_remote_copy(
            src_ref=src, dst_ref=dst, send_sem=ssem, recv_sem=rsem, device_id=dev, device_id_type=MESH
        )

    half = pl.ds(pl.multiple_of(c * 256, 256), 256)
    other = pl.ds(pl.multiple_of((1 - c) * 256, 256), 256)
    loads = [pltpu.make_async_copy(grad.at[:, half], go, s_in.at[0])]
    loads += [
        pltpu.make_async_copy(src, dst, s_in.at[1 + i])
        for i, (src, dst) in enumerate(
            ((basis_l, ql), (basis_r, qr), (stats_l, sl), (stats_r, sr), (mom1, m1), (mom2, m2))
        )
    ]
    swaps = []
    for i, k in enumerate((1, 3, 4)):
        for h in range(2):
            swaps.append(
                pltpu.make_async_copy(
                    basis_r.at[k, :, h], qrs.at[i, :, 1 - h], s_in.at[7 + 2 * i + h]
                )
            )
    loads[0].start()

    barrier = pltpu.get_barrier_semaphore()
    for d in range(1, 16):
        pl.semaphore_signal(barrier, inc=1, device_id=(lax.rem(rep + d, 16), own), device_id_type=MESH)
    for d in range(1, NZ):
        pl.semaphore_signal(barrier, inc=1, device_id=at_z(lax.rem(z + d, NZ)), device_id_type=MESH)
    for d in range(1, NX):
        pl.semaphore_signal(barrier, inc=1, device_id=at_x(lax.rem(x + d, NX)), device_id_type=MESH)
    pl.semaphore_wait(barrier, 15 + NZ - 1 + NX - 1)

    def core_copy(j):
        rows = pl.ds(j * 384, 384)
        return remote(grad.at[rows, other], gx.at[rows], s_core.at[j], r_core.at[j], sib)

    for j in range(3):
        core_copy(j).start()
    for d in loads[1:] + swaps:
        d.start()
    out_of = iota((128, 1), 0)
    perm1 = onehot(iota((128, 128), 1), (out_of % 16) * 8 + out_of // 16)
    loads[0].wait()
    for j in range(3):
        core_copy(j).wait_recv()
        for g in range(3 * j, 3 * j + 3):
            rows = pl.ds(g * 128, 128)
            both = (mm(perm1, go[rows, :]) + mm(perm1, gx[rows, :])).astype(BF)
            for t in range(NY):
                chunk[t, pl.ds(g * 16, 16), :] = both[t * 16 : t * 16 + 16]

    def rs_copy(d, s, j):
        rows = pl.ds(j * SUBROWS, SUBROWS)
        sign = 1 - 2 * d
        if s == 0:
            lanes = pl.ds(d * 128, 128)
            src = chunk.at[lax.rem(y + 4, NY), rows, lanes]
            dst = rs_recv.at[d, s, rows, lanes]
        else:
            src = rs_send.at[d, s - 1, rows]
            dst = rs_recv.at[d, s, rows]
        return remote(src, dst, s_rs.at[d, s, j], r_rs.at[d, s, j], at_y(y + sign, c))

    def rs_step(s):
        for j in range(SUBS):
            for d in range(2):
                rows = pl.ds(j * SUBROWS, SUBROWS)
                t = lax.rem(y + (1 - 2 * d) * (4 - s) + NY, NY)
                rs_copy(d, s - 1, j).wait_recv()
                if s == 1:
                    lanes = pl.ds(d * 128, 128)
                    rest = pl.ds((1 - d) * 128, 128)
                    rs_send[d, 0, rows, lanes] = (
                        chunk[t, rows, lanes].astype(F32) + rs_recv[d, 0, rows, lanes].astype(F32)
                    ).astype(BF)
                    rs_send[d, 0, rows, rest] = chunk[t, rows, rest]
                else:
                    rs_send[d, s - 1, rows] = (
                        chunk[t, rows].astype(F32) + rs_recv[d, s - 1, rows].astype(F32)
                    ).astype(BF)
                rs_copy(d, s, j).start()

    for j in range(SUBS):
        for d in range(2):
            rs_copy(d, 0, j).start()

    o_row = own_row[...]
    e_row = onehot(iota((128, PADB), 0), o_row)
    before = mm(e_row, onehot_lt(iota((PADB, PADB), 0), iota((PADB, PADB), 1)))
    k_row = jnp.sum(before * e_row.astype(F32), axis=0, keepdims=True).astype(jnp.int32)
    zr, xr = o_row >> 2, o_row & 3
    code = jnp.where((zr >> 3) == c, (k_row * 8 + (zr & 7)) * 16 + xr, -64)
    for q in range(4):
        place[q] = onehot(iota((640, PADB), 0), code + 4 * q)
    summed[:, pl.ds(NB, PADB - NB), :] = jnp.zeros((2, PADB - NB, 256), BF)
    rs_step(1)

    o_col = own_col[...]
    e_col = onehot(iota((PADB, 128), 1), o_col)
    before = mm(onehot_lt(iota((PADB, PADB), 1), iota((PADB, PADB), 0)), e_col)
    k_col = jnp.sum(before * e_col.astype(F32), axis=1, keepdims=True).astype(jnp.int32)
    zc, xc = o_col >> 2, o_col & 3
    ohfin[...] = onehot(iota((NB, 256), 1), ((k_col >> 1) * 64 + xc * 16 + zc)[:NB])
    upper = ((k_col + y) & 1)[:NB]
    rho = iota((1, 512), 1)
    natural = ((rho & 15) * 4 + ((rho >> 4) & 3)) * 8 + (rho >> 6)
    pm[...] = onehot(iota((512, 512), 0), natural)
    rs_step(2)

    for d in loads[1:] + swaps:
        d.wait()
    mine = onehot(iota((32, 512), 1), iota((32, 512), 0) + rep * 32)
    for k in range(SLOTS):
        arot[k] = mm(mm_t(mine, ql[k]).astype(BF), pm[...]).astype(BF)
    rs_step(3)

    j2 = iota((256, 1), 0)
    perm2[...] = onehot(iota((256, 256), 1), (j2 & 15) * 16 + ((j2 >> 4) & 3) * 4 + (j2 >> 6))
    j3 = iota((512, 1), 0)
    perm3[...] = onehot(
        iota((512, 512), 1), (j3 & 15) * 32 + (j3 >> 7) * 8 + ((j3 >> 4) & 7)
    )
    for j in range(SUBS):
        rows = pl.ds(j * SUBROWS, SUBROWS)
        for d in range(2):
            rs_copy(d, 3, j).wait_recv()
        summed[c, rows] = (
            chunk[y, rows].astype(F32) + rs_recv[0, 3, rows].astype(F32) + rs_recv[1, 3, rows].astype(F32)
        ).astype(BF)
    to_sib = remote(
        summed.at[c, pl.ds(0, NB)], summed.at[c, pl.ds(0, NB)], s_cag.at[0], r_cag.at[0], sib
    )
    to_sib.start()
    from_sib = remote(
        summed.at[1 - c, pl.ds(0, NB)], summed.at[1 - c, pl.ds(0, NB)], s_cag.at[0], r_cag.at[0], sib
    )
    from_sib.wait_recv()

    placed = mm(place[0], summed[0, :, pl.ds(0, 128)])
    placed += mm(place[1], summed[0, :, pl.ds(128, 128)])
    placed += mm(place[2], summed[1, :, pl.ds(0, 128)])
    placed += mm(place[3], summed[1, :, pl.ds(128, 128)])
    v1[...] = placed.astype(BF).reshape(SLOTS, 8, 16, 128)

    def z1_copy(j):
        low = lax.rem(z + j, 8)
        return remote(v1.at[:, low], w1.at[:, z], s_z1.at[j], r_z1.at[z], at_z(c * 8 + low))

    for j in range(1, 8):
        z1_copy(j).start()

    @pl.when(jnp.logical_not(active))
    def _():
        z1_copy(0).start()

    @pl.when(active)
    def _():
        w1[:, z] = v1[:, lax.rem(z, 8)]

    def ag_copy(d, s, k):
        sign = 1 - 2 * d
        origin = lax.rem(y - sign * s + NY, NY)
        rows = pl.ds(pl.multiple_of(origin * 64, 64), 64)
        ref = gall.at[k, rows] if s < 3 else gall.at[k, rows, pl.ds(d * 256, 256)]
        return remote(ref, ref, s_ag.at[d, s, k], r_ag.at[d, s, k], at_y(y + sign, c))

    def ag_arrival(d, s, k):
        sign = 1 - 2 * d
        origin = lax.rem(y - sign * (s + 1) + NY, NY)
        rows = pl.ds(pl.multiple_of(origin * 64, 64), 64)
        return gall.at[k, rows] if s < 3 else gall.at[k, rows, pl.ds(d * 256, 256)]

    def ag_wait(d, s, k):
        ref = ag_arrival(d, s, k)
        remote(ref, ref, s_ag.at[d, s, k], r_ag.at[d, s, k], at_y(y, c)).wait_recv()

    def sib_copy(i, k):
        if i == 8:
            ref = gall.at[k, pl.ds(pl.multiple_of(y * 64, 64), 64)]
        else:
            ref = ag_arrival(i // 4, i % 4, k)
        return remote(ref, ref, s_sib.at[i, k], r_sib.at[i, k], sib)

    def x1_copy(j):
        to = lax.rem(x + j, NX)
        rows = pl.ds(pl.multiple_of(y * 64 + x * 16, 16), 16)
        return remote(xs1.at[:, to], gall.at[:, rows], s_x1.at[j - 1], r_x1.at[x], at_x(to))

    def x1_wait(j):
        src = lax.rem(x + j, NX)
        rows = pl.ds(pl.multiple_of(y * 64 + src * 16, 16), 16)
        remote(xs1.at[:, src], gall.at[:, rows], s_x1.at[0], r_x1.at[src], at_x(src)).wait_recv()

    @pl.when(active)
    def _():
        for j in range(1, NZ):
            src = lax.rem(z + j, NZ)
            remote(v1.at[:, 0], w1.at[:, src], s_z1.at[0], r_z1.at[src], at_z(src)).wait_recv()
        for k in range(SLOTS):
            regrouped = mm(perm2[...], w1[k].reshape(256, 128)).astype(BF)
            for to in range(NX):
                for q in range(4):
                    n = (to * 4 + q) * 16
                    xs1[k, to, :, pl.ds(q * 128, 128)] = regrouped[n : n + 16]
        for j in range(1, NX):
            x1_copy(j).start()
        for k in range(SLOTS):
            gall[k, pl.ds(pl.multiple_of(y * 64 + x * 16, 16), 16), :] = xs1[k, x]
        for j in range(1, NX):
            x1_wait(j)

    lane_low = iota((32, 128), 1) < 64
    back = {}

    def slot_products(k):
        h = mm(arot[k], gall[k]).astype(BF)
        rotated = mm(h, qr[k].reshape(512, 512))
        first = BETA_FIRST * m1[k] + (1.0 - BETA_FIRST) * rotated
        second = BETA_SECOND * m2[k] + (1.0 - BETA_SECOND) * rotated * rotated
        out_1[k] = first
        out_2[k] = second
        direction = (first / (jnp.sqrt(second) + EPSILON)).astype(BF)
        if k in (0, 2, 4):
            back[k, 0] = mm_t(direction, qr[k].reshape(512, 512)).astype(BF)
        if k in (1, 3, 4):
            back[k, 1] = mm_t(direction, qrs[(k - 1) // 2 if k < 4 else 2].reshape(512, 512)).astype(BF)

    def b_copy(p, yy):
        return remote(bmsg.at[p, yy], bb.at[p, rep], s_b.at[p, yy], r_b.at[p, rep], (yy * 2 + PAIR_CORE[p], own))

    def send_back(p):
        a, b = PAIRS[p]
        for yy in range(NY):
            lanes = slice((yy // 2) * 128, (yy // 2) * 128 + 128)
            lo, hi = back[a, 0][:, lanes], back[b, 1][:, lanes]
            bmsg[p, yy] = jnp.where(lane_low, lo, hi) if yy % 2 == 0 else jnp.where(lane_low, hi, lo)
        for yy in range(NY):
            here = jnp.logical_and(yy == y, c == PAIR_CORE[p])

            @pl.when(jnp.logical_not(here))
            def _():
                b_copy(p, yy).start()

            @pl.when(here)
            def _():
                bb[p, rep] = bmsg[p, yy]

    def stat_products(k):
        columns = mm_t(mine, gall[k]).astype(BF)
        right = mm(columns, gall[k])
        out_r[k] = (BETA_SECOND * sr[k].astype(F32) + (1.0 - BETA_SECOND) * right).astype(BF)
        rows = mm(pm[pl.ds(pl.multiple_of(rep * 32, 32), 32), :], gall[k]).astype(BF)
        left = mm_t(rows, gall[k])
        high = left.astype(BF)
        low = (left - high.astype(F32)).astype(BF)
        left = mm_t(high, pm[...]) + mm_t(low, pm[...])
        out_l[k] = (BETA_SECOND * sl[k].astype(F32) + (1.0 - BETA_SECOND) * left).astype(BF)

    for w in range(SLOTS + 4):

        @pl.when(active)
        def _():
            for s in range(4, -1, -1):
                k = w - s
                if k < 0 or k >= SLOTS:
                    continue
                for d in range(2):
                    if s > 0:
                        ag_wait(d, s - 1, k)
                    if s < 4:
                        ag_copy(d, s, k).start()
                    if s > 0:
                        sib_copy(d * 4 + s - 1, k).start()
                if s == 0:
                    sib_copy(8, k).start()

        if w >= 4:
            k = w - 4

            @pl.when(jnp.logical_not(active))
            def _():
                for i in range(8):
                    ref = ag_arrival(i // 4, i % 4, k)
                    remote(ref, ref, s_sib.at[i, k], r_sib.at[i, k], sib).wait_recv()
                sib_copy(8, k).wait_recv()

            slot_products(k)
            if k in (1, 3, 4):
                send_back((1, 3, 4).index(k))

    for i in range(8):
        j = iota((256, 256), 1)
        l = iota((256, 256), 0)
        wanted = (l & 64) == ((l >> 7) << 6)
        pick[i] = jnp.where(
            ((l & 63) == (j & 31) + 32 * c) & wanted & ((j >> 5) == i), 1.0, 0.0
        ).astype(BF)
    yb[pl.ds(3, 1)] = jnp.zeros((1, NX, 8, 16, 128), BF)

    def z2_copy(p, j):
        to = lax.rem(z + j, NZ)
        return remote(
            ub.at[p, pl.ds(pl.multiple_of(to * 32, 32), 32)], w2.at[p, z], s_z2.at[p, j - 1], r_z2.at[p, z], at_z(to)
        )

    def x2_copy(p, j):
        to = lax.rem(x + j, NX)
        return remote(xs2.at[p, to], yb.at[p, x], s_x2.at[p, j - 1], r_x2.at[p, x], at_x(to))

    def y_copy(p):
        return remote(yb.at[p], yb.at[p], s_y.at[p], r_y.at[p], sib)

    def update_products(p):
        for d in range(1, 16):
            src = lax.rem(rep + d, 16)
            remote(bmsg.at[p, 0], bb.at[p, src], s_b.at[p, 0], r_b.at[p, src], (src, own)).wait_recv()
        a, b = PAIRS[p]
        columns = bb[p].reshape(512, 128)
        if a == b:
            ub[p] = mm(ql[a], columns).astype(BF)
        else:
            swap = jnp.where(iota((512, 128), 1) < 64, 0, 1) == (y & 1)
            ub[p] = jnp.where(swap, mm(ql[a], columns), mm(ql[b], columns)).astype(BF)
        for j in range(1, NZ):
            z2_copy(p, j).start()
        w2[p, z] = ub[p, pl.ds(pl.multiple_of(z * 32, 32), 32)]

    def update_regroup(p):
        for j in range(1, NZ):
            src = lax.rem(z + j, NZ)
            remote(ub.at[p, pl.ds(0, 32)], w2.at[p, src], s_z2.at[p, 0], r_z2.at[p, src], at_z(src)).wait_recv()
        xs2[p] = mm(perm3[...], w2[p].reshape(512, 128)).astype(BF).reshape(NX, 8, 16, 128)
        for j in range(1, NX):
            x2_copy(p, j).start()
        yb[p, x] = xs2[p, x]

    def update_share(p):
        for j in range(1, NX):
            src = lax.rem(x + j, NX)
            remote(xs2.at[p, 0], yb.at[p, src], s_x2.at[p, 0], r_x2.at[p, src], at_x(src)).wait_recv()
        y_copy(p).start()

    for core in range(2):
        mine_of = [p for p in range(3) if PAIR_CORE[p] == core]

        @pl.when(c == core)
        def _():
            for p in mine_of:
                update_products(p)
            for k in range(SLOTS):
                stat_products(k)
            for p in mine_of:
                update_regroup(p)
            for p in mine_of:
                update_share(p)
            for p in range(3):
                if PAIR_CORE[p] != core:
                    y_copy(p).wait_recv()

    upper_f = upper.astype(F32)
    total = jnp.zeros((NB, 256), F32)
    for i in range(8):
        rows = yb[:, :, i].reshape(256, 128)
        found = mm(ohfin[...], rows)
        both = jnp.concatenate([found * (1.0 - upper_f), found * upper_f], axis=1).astype(BF)
        total += mm(both, pick[i])
    out_u[...] = total.astype(BF)

    for j in range(3):
        core_copy(j).wait_send()
    for s in range(4):
        for j in range(SUBS):
            for d in range(2):
                rs_copy(d, s, j).wait_send()
    to_sib.wait_send()
    for j in range(1, 8):
        z1_copy(j).wait_send()

    @pl.when(jnp.logical_not(active))
    def _():
        z1_copy(0).wait_send()

    @pl.when(active)
    def _():
        for j in range(1, NX):
            x1_copy(j).wait_send()
        for k in range(SLOTS):
            for s in range(4):
                for d in range(2):
                    ag_copy(d, s, k).wait_send()
                    sib_copy(d * 4 + s, k).wait_send()
            sib_copy(8, k).wait_send()

    for p in range(3):
        for yy in range(NY):

            @pl.when(jnp.logical_not(jnp.logical_and(yy == y, c == PAIR_CORE[p])))
            def _():
                b_copy(p, yy).wait_send()

        @pl.when(c == PAIR_CORE[p])
        def _():
            for j in range(1, NZ):
                z2_copy(p, j).wait_send()
            for j in range(1, NX):
                x2_copy(p, j).wait_send()
            y_copy(p).wait_send()


def onehot_lt(a, b):
    return jnp.where(a < b, 1.0, 0.0).astype(BF)


def shards(grad_parts, owner_of, stats_left, stats_right, basis_left, basis_right, moment_first, moment_second):
    blocks = owner_of.shape[0]
    padded = jnp.pad(owner_of[:, 0], (0, PADB - blocks), constant_values=-1)
    anywhere = pl.BlockSpec(memory_space=pl.ANY)
    vmem = pl.BlockSpec(memory_space=pltpu.VMEM)
    rows = (SLOTS, 32, 512)
    dma = pltpu.SemaphoreType.DMA
    scratch = [
        pltpu.VMEM((1152, 256), BF),
        pltpu.VMEM((1152, 256), BF),
        pltpu.VMEM((NY, NB, 256), BF),
        pltpu.VMEM((2, 4, NB, 256), BF),
        pltpu.VMEM((2, 3, NB, 256), BF),
        pltpu.VMEM((2, PADB, 256), BF),
        pltpu.VMEM((4, 640, PADB), BF),
        pltpu.VMEM((SLOTS, 8, 16, 128), BF),
        pltpu.VMEM((SLOTS, NZ, 16, 128), BF),
        pltpu.VMEM((SLOTS, NX, 16, 512), BF),
        pltpu.VMEM((SLOTS, 512, 512), BF),
        pltpu.VMEM((SLOTS, 512, 512), BF),
        pltpu.VMEM((SLOTS, 4, 2, 64, 512), BF),
        pltpu.VMEM((3, 4, 2, 64, 512), BF),
        pltpu.VMEM(rows, BF),
        pltpu.VMEM(rows, BF),
        pltpu.VMEM(rows, F32),
        pltpu.VMEM(rows, F32),
        pltpu.VMEM(rows, BF),
        pltpu.VMEM((512, 512), BF),
        pltpu.VMEM((256, 256), BF),
        pltpu.VMEM((512, 512), BF),
        pltpu.VMEM((NB, 256), BF),
        pltpu.VMEM((8, 256, 256), BF),
        pltpu.VMEM((3, NY, 32, 128), BF),
        pltpu.VMEM((3, 16, 32, 128), BF),
        pltpu.VMEM((3, 512, 128), BF),
        pltpu.VMEM((3, NZ, 32, 128), BF),
        pltpu.VMEM((3, NX, 8, 16, 128), BF),
        pltpu.VMEM((4, NX, 8, 16, 128), BF),
        dma((13,)),
        dma((3,)), dma((3,)),
        dma((2, 4, SUBS)), dma((2, 4, SUBS)),
        dma((1,)), dma((1,)),
        dma((8,)), dma((NZ,)),
        dma((3,)), dma((NX,)),
        dma((2, 4, SLOTS)), dma((2, 4, SLOTS)),
        dma((9, SLOTS)), dma((9, SLOTS)),
        dma((3, NY)), dma((3, 16)),
        dma((3, NZ - 1)), dma((3, NZ)),
        dma((3, NX - 1)), dma((3, NX)),
        dma((3,)), dma((3,)),
    ]
    new_left, new_right, new_first, new_second, picked = pl.pallas_call(
        kernel,
        out_shape=(
            jax.ShapeDtypeStruct(rows, BF),
            jax.ShapeDtypeStruct(rows, BF),
            jax.ShapeDtypeStruct(rows, F32),
            jax.ShapeDtypeStruct(rows, F32),
            jax.ShapeDtypeStruct((blocks, 256), BF),
        ),
        in_specs=[anywhere, vmem, vmem] + [anywhere] * 6,
        out_specs=(vmem,) * 5,
        scratch_shapes=scratch,
        compiler_params=pltpu.CompilerParams(
            collective_id=0, has_side_effects=True, vmem_limit_bytes=56 * 1024 * 1024
        ),
    )(
        grad_parts[0].reshape(blocks * 8, 512),
        padded[:, None],
        padded[None, :],
        stats_left[0],
        stats_right[0],
        basis_left[0],
        basis_right[0].reshape(SLOTS, 4, 2, 64, 512),
        moment_first[0],
        moment_second[0],
    )
    update = picked.reshape(blocks, 8, 32)
    return (new_left[None], new_right[None], new_first[None], new_second[None], update)


def solution(mesh):
    return jax.shard_map(
        shards,
        mesh=mesh,
        in_specs=(
            P("replica", None, "owner", None),
            P(),
            P("owner", None, "replica", None),
            P("owner", None, "replica", None),
            P("owner", None, None, None),
            P("owner", None, None, None),
            P("owner", None, "replica", None),
            P("owner", None, "replica", None),
        ),
        out_specs=(
            P("owner", None, "replica", None),
            P("owner", None, "replica", None),
            P("owner", None, "replica", None),
            P("owner", None, "replica", None),
            P(None, "owner", "replica"),
        ),
        check_vma=False,
    )
```

time: 270 us -> 125 us (0.46)
  waiting for transfers between devices: 181 us -> 0 us
  Pallas kernels: 0 us -> 114 us
  blocking collectives: 30.9 us -> 0 us
  starting transfers between devices: 16.2 us -> 0 us
  matrix products: 14.4 us -> 0 us
  between operations: 13.9 us -> 0.64 us
    pallas_call x0 -> x1, Pallas kernels: none -> 114 us  [shards(): pl.pallas_call(kernel, out_shape=(jax.ShapeDtypeStruct(rows, BF), jax.Sha...]
    all_gather x2 -> x0, waiting for transfers between devices: 91.3 us -> none  [the longest x1 47.3 us: shards(): all_rows = lax.all_gather(direction, 'replica', axis=1, tiled=True)]
    reduce_scatter x1 -> x0, waiting for transfers between devices: 74.3 us -> none  [shards(): lax.psum_scatter(grad_parts[0].astype(jnp.float32).astype(jnp.bfloat16),...]
    all_to_all x1 -> x0, blocking collectives: 30.9 us -> none  [shards(): lax.all_to_all(outgoing, 'owner', split_axis=1, concat_axis=1, tiled=True)]
    all_to_all x1 -> x0, starting transfers between devices: 16.1 us -> none  [shards(): lax.all_to_all(leaving, 'owner', split_axis=1, concat_axis=1, tiled=True)]
    all_to_all x1 -> x0, waiting for transfers between devices: 15.2 us -> none  [shards(): lax.all_to_all(leaving, 'owner', split_axis=1, concat_axis=1, tiled=True)]
    dot_general x6 -> x0, matrix products: 14.4 us -> none  [the longest x1 4.65 us: shards(): jnp.einsum('sic,scj->sij', half_rot, right_basis, preferred_element_type=...]
    reshape x5 -> x0, local copies, waits for them, and re-layouts: 3.63 us -> none  [the longest x2 2.38 us: shards(): update_cols.reshape(slot_count, owners_count, row_width * slab_width)]
  transfers between devices with their start and end apart: 4 -> 0, of which waited for: 4 -> 0; matrix products, arithmetic and copies ran while one was open for 2% -> 0% of each run, Pallas kernels for 0% -> 0%
where the time goes in v1:
time: 125 us; the launch traced here: 124 us
  Pallas kernels  114 us (91%)
  local copies, waits for them, and re-layouts  9.76 us (8%)
    pallas_call x1, Pallas kernels, shards(): pl.pallas_call(kernel, out_shape=(jax.ShapeDtypeStruct(rows, BF), jax.Sha...  114 us
    unnamed x6, local copies, waits for them, and re-layouts  6.63 us

profile of v1, /device:TPU:1, one launch (start us, length us, event | category | flops | bytes accessed | tf_op | source)
XLA Modules:
  0.0 124.4 jit_solution(13267561181768847213)
XLA Ops:
  0.6 0.7 pad.4
  1.3 0.0 copy-start
  1.3 0.8 copy.14.own_col
  2.1 0.0 copy-done
  2.1 113.9 %shard_map.119 = (bf16[5,32,512]{2,1,0:T(8,128)(2,1)}, bf16[5,32,512]{2,1,0:T(8,128)(2,1)}, f32[5,32,512]{2,1,0:T(8,128)}, f32[5,32,512]{2,1,0:T(8,128)}, bf16[144,256]{1,0:T(8,128)(2,1)}) custom-call(bf16[1152,512]{1,0:T(8,128)(2,1)} %bitcast.17, s32[256,1]{1,0:T(8,128)} %copy.14.own_col, s32[1,256]{1,0:T(1,128)} %bitcast.28, bf16[5,32,512]{2,1,0:T(8,128)(2,1)} %bitcast.24, ...), custom_call_target="tpu_custom_call" | custom-call | tf_op jit(solution)/shard_map/pallas_call | solution.py:529
  116.1 1.6 %copy.15 = bf16[144,256]{0,1:T(8,128)(2,1)} copy(bf16[144,256]{1,0:T(8,128)(2,1)} %get-tuple-element.14) | data formatting | bytes 147456 | tf_op jit(solution)/shard_map/pallas_call | solution.py:529
  117.7 1.6 %copy.20 = bf16[1,5,32,512]{3,2,1,0:T(8,128)(2,1)} copy(bf16[1,5,32,512]{3,2,1,0:T(8,128)(2,1)} %bitcast.23) | data formatting | bytes 327680
  119.3 1.6 %copy.21 = bf16[1,5,32,512]{3,2,1,0:T(8,128)(2,1)} copy(bf16[1,5,32,512]{3,2,1,0:T(8,128)(2,1)} %bitcast.22) | data formatting | bytes 327680
  120.9 1.7 %copy.22 = f32[1,5,32,512]{3,2,1,0:T(8,128)} copy(f32[1,5,32,512]{3,2,1,0:T(8,128)} %bitcast.21) | data formatting | bytes 655360
  122.6 1.7 %copy.23 = f32[1,5,32,512]{3,2,1,0:T(8,128)} copy(f32[1,5,32,512]{3,2,1,0:T(8,128)} %bitcast.20) | data formatting | bytes 655360
Async XLA Ops:
  1.3 0.8 copy-start

commit v2 on v0

v2 whole, which is shorter than its diff:
```python
import jax
import jax.numpy as jnp
from jax import lax
from jax.experimental import pallas as pl
from jax.experimental.pallas import tpu as pltpu
from jax.sharding import PartitionSpec as P

BETA_FIRST = 0.9
BETA_SECOND = 0.95
EPSILON = 1e-08
MESH = pl.DeviceIdType.MESH
BF = jnp.bfloat16
F32 = jnp.float32
NY, NX, NZ = 8, 4, 16
NB, PADB = 144, 256
SLOTS = 5
SUBS, SUBROWS = 3, 48
PAIRS = ((0, 1), (2, 3), (4, 4))
PAIR_CORE = (0, 1, 0)


def mm(a, b):
    return jnp.dot(a, b, preferred_element_type=F32)


def mm_t(a, b):
    return lax.dot_general(a, b, (((1,), (1,)), ((), ())), preferred_element_type=F32)


def iota(shape, axis):
    return lax.broadcasted_iota(jnp.int32, shape, axis)


def onehot(a, b):
    return jnp.where(a == b, 1.0, 0.0).astype(BF)


def kernel(
    grad, own_row, stats_l, stats_r, basis_l, basis_r, mom1, mom2,
    out_l, out_r, out_1, out_2, out_u,
    go, gx, chunk, rs_recv, rs_send, summed, place, v1, w1, xs1, gall,
    ql, qr, qrs, sl, sr, m1, m2, ol, orr, o1, o2, qlt, hsend, hrecv, gf, pm, perm2, perm3, perm4, oh2, wbuf,
    bmsg, bb, ub, ub4, w2, w24, xs2, yb,
    s_in, s_out, s_core, r_core, s_rs, r_rs, s_cag, r_cag, s_z1, r_z1, s_x1, r_x1,
    s_h, r_h, s_own, r_own, s_ag, r_ag, s_sib, r_sib, s_b, r_b, s_z2, r_z2, s_x2, r_x2, s_y, r_y,
):
    rep = lax.axis_index("replica")
    own = lax.axis_index("owner")
    y, c = rep // 2, rep % 2
    z, x = own // NX, own % NX
    sib = (y * 2 + (1 - c), own)
    zhalf = z // 8
    active = c == zhalf

    def at_y(yy, cc):
        return (lax.rem(yy + 2 * NY, NY) * 2 + cc, own)

    def at_z(zz):
        return (rep, zz * NX + x)

    def at_x(xx):
        return (rep, z * NX + xx)

    def remote(src, dst, ssem, rsem, dev):
        return pltpu.make_async_remote_copy(
            src_ref=src, dst_ref=dst, send_sem=ssem, recv_sem=rsem, device_id=dev, device_id_type=MESH
        )

    half = pl.ds(pl.multiple_of(c * 256, 256), 256)
    other = pl.ds(pl.multiple_of((1 - c) * 256, 256), 256)
    loads = [pltpu.make_async_copy(grad.at[:, half], go, s_in.at[0])]
    loads += [
        pltpu.make_async_copy(src, dst, s_in.at[1 + i])
        for i, (src, dst) in enumerate(
            ((basis_l, ql), (basis_r, qr), (stats_l, sl), (stats_r, sr), (mom1, m1), (mom2, m2))
        )
    ]
    swaps = []
    for i, k in enumerate((1, 3, 4)):
        for h in range(2):
            swaps.append(
                pltpu.make_async_copy(
                    basis_r.at[k, :, h], qrs.at[i, :, 1 - h], s_in.at[7 + 2 * i + h]
                )
            )
    loads[0].start()
    drains = []

    barrier = pltpu.get_barrier_semaphore()
    for d in range(1, 16):
        pl.semaphore_signal(barrier, inc=1, device_id=(lax.rem(rep + d, 16), own), device_id_type=MESH)
    for d in range(1, NZ):
        pl.semaphore_signal(barrier, inc=1, device_id=at_z(lax.rem(z + d, NZ)), device_id_type=MESH)
    for d in range(1, NX):
        pl.semaphore_signal(barrier, inc=1, device_id=at_x(lax.rem(x + d, NX)), device_id_type=MESH)
    pl.semaphore_wait(barrier, 15 + NZ - 1 + NX - 1)

    def core_copy(j):
        rows = pl.ds(j * 384, 384)
        return remote(grad.at[rows, other], gx.at[rows], s_core.at[j], r_core.at[j], sib)

    def rs_target(d, s):
        t = lax.rem(y + (1 - 2 * d) * (4 - s) + NY, NY)
        return (t // 4) * 2 + t % 2, c == (t % 4) // 2

    def rs_copy(d, s, j):
        rows = pl.ds(j * SUBROWS, SUBROWS)
        if s == 0:
            lanes = pl.ds(d * 256, 256)
            src = chunk.at[rs_target(d, 0)[0], rows, lanes]
            dst = rs_recv.at[d, s, rows, lanes]
        else:
            src = rs_send.at[d, s - 1, rows]
            dst = rs_recv.at[d, s, rows]
        return remote(src, dst, s_rs.at[d, s, j], r_rs.at[d, s, j], at_y(y + 1 - 2 * d, c))

    for j in range(3):
        core_copy(j).start()
    for d in loads[1:] + swaps:
        d.start()

    out_of = iota((128, 1), 0)
    perm1 = onehot(iota((128, 128), 1), (out_of % 16) * 8 + out_of // 16)
    o_row = own_row[...]
    e_row = onehot(iota((128, PADB), 0), o_row)
    before = mm(e_row, onehot_lt(iota((PADB, PADB), 0), iota((PADB, PADB), 1)))
    k_row = jnp.sum(before * e_row.astype(F32), axis=0, keepdims=True).astype(jnp.int32)
    zr, xr = o_row >> 2, o_row & 3
    code = jnp.where((zr >> 3) == c, (k_row * 8 + (zr & 7)) * 16 + xr, -64)
    for q in range(4):
        place[q] = onehot(iota((640, PADB), 0), code + 4 * q)
    side = jnp.where(k_row == 4, x >> 1, (k_row + y) & 1)
    slot_code = side * 256 + (k_row >> 1) * 64 + xr * 16 + zr
    summed[pl.ds(NB, PADB - NB), :] = jnp.zeros((PADB - NB, 512), BF)

    loads[0].wait()
    for j in range(3):
        core_copy(j).wait_recv()
        for g in range(3 * j, 3 * j + 3):
            rows = pl.ds(g * 128, 128)
            both = (mm(perm1, go[rows, :]) + mm(perm1, gx[rows, :])).astype(BF)
            for i in range(8):
                for q in range(2):
                    chunk[(i // 4) * 2 + q, pl.ds(g * 16, 16), pl.ds((i % 4) * 128, 128)] = both[
                        i * 16 : i * 16 + 16, q * 128 : q * 128 + 128
                    ]

        @pl.when(rs_target(0, 0)[1])
        def _():
            for d in range(2):
                rs_copy(d, 0, j).start()

    drains.append(lambda: [core_copy(j).wait_send() for j in range(3)])

    for d in loads[1:] + swaps:
        d.wait()
    r_col = iota((256, 1), 0)
    held = ((r_col & 15) * 4 + ((r_col >> 4) & 3)) * 8 + (y // 4) * 4 + (r_col >> 6)
    held_rows = onehot(iota((256, 512), 1), held)
    same = onehot(iota((512, 512), 0), iota((512, 512), 1))

    def turn_basis(k):
        qlt[k] = mm_t(same, mm(held_rows, ql[k]).astype(BF)).astype(BF)

    turn_basis(0)

    for s in range(1, 4):
        for j in range(SUBS):
            for d in range(2):
                rows = pl.ds(j * SUBROWS, SUBROWS)
                t, here = rs_target(d, s)

                @pl.when(here)
                def _():
                    rs_copy(d, s - 1, j).wait_recv()
                    if s == 1:
                        lanes = pl.ds(d * 256, 256)
                        rest = pl.ds((1 - d) * 256, 256)
                        rs_send[d, 0, rows, lanes] = (
                            chunk[t, rows, lanes].astype(F32) + rs_recv[d, 0, rows, lanes].astype(F32)
                        ).astype(BF)
                        rs_send[d, 0, rows, rest] = chunk[t, rows, rest]
                    else:
                        rs_send[d, s - 1, rows] = (
                            chunk[t, rows].astype(F32) + rs_recv[d, s - 1, rows].astype(F32)
                        ).astype(BF)
                    rs_copy(d, s, j).start()

        if s == 1:
            turn_basis(1)
            turn_basis(2)
        if s == 2:
            turn_basis(3)
            turn_basis(4)
        if s == 3:
            j2 = iota((256, 1), 0)
            perm2[...] = onehot(iota((256, 256), 1), (j2 & 15) * 16 + ((j2 >> 4) & 3) * 4 + (j2 >> 6))
            rho = iota((1, 512), 1)
            natural = ((rho & 15) * 4 + ((rho >> 4) & 3)) * 8 + (rho >> 8) * 4 + ((rho >> 6) & 3)
            pm[...] = onehot(iota((512, 512), 0), natural)

    def share_sum(j):
        ref = summed.at[pl.ds(j * SUBROWS, SUBROWS)]
        return remote(ref, ref, s_cag.at[j], r_cag.at[j], sib)

    last, sums_here = rs_target(0, 4)

    @pl.when(sums_here)
    def _():
        for j in range(SUBS):
            rows = pl.ds(j * SUBROWS, SUBROWS)
            for d in range(2):
                rs_copy(d, 3, j).wait_recv()
            summed[rows] = (
                chunk[last, rows].astype(F32) + rs_recv[0, 3, rows].astype(F32) + rs_recv[1, 3, rows].astype(F32)
            ).astype(BF)
            share_sum(j).start()

    @pl.when(jnp.logical_not(sums_here))
    def _():
        for j in range(SUBS):
            share_sum(j).wait_recv()

    def drain_2():
        for s in range(4):
            for d in range(2):

                @pl.when(rs_target(d, s)[1])
                def _():
                    for j in range(SUBS):
                        rs_copy(d, s, j).wait_send()

        @pl.when(sums_here)
        def _():
            for j in range(SUBS):
                share_sum(j).wait_send()

    drains.append(drain_2)

    def z1_copy(k, j):
        low = lax.rem(z + j + 4 * active.astype(jnp.int32), 8)
        return remote(v1.at[k, low], w1.at[k, z], s_z1.at[k, j], r_z1.at[k, z], at_z(c * 8 + low))

    def fill_slots(k, n):
        rows = pl.ds(k * 128, n * 128)
        placed = mm(place[0, rows], summed[:, pl.ds(0, 128)])
        for q in range(1, 4):
            placed += mm(place[q, rows], summed[:, pl.ds(q * 128, 128)])
        v1[pl.ds(k, n)] = placed.astype(BF).reshape(n, 8, 16, 128)
        for kk in range(k, k + n):
            for j in (0, 1, 7, 2, 6, 3, 5):
                z1_copy(kk, j).start()

            @pl.when(jnp.logical_not(active))
            def _():
                z1_copy(kk, 4).start()

        @pl.when(active)
        def _():
            w1[pl.ds(k, n), z] = v1[pl.ds(k, n), lax.rem(z, 8)]

    fill_slots(0, 1)
    fill_slots(1, 4)

    def drain_3():
        for k in range(SLOTS):
            for j in (0, 1, 7, 2, 6, 3, 5):
                z1_copy(k, j).wait_send()

        @pl.when(jnp.logical_not(active))
        def _():
            for k in range(SLOTS):
                z1_copy(k, 4).wait_send()

        @pl.when(active)
        def _():
            for k in range(SLOTS):
                for j in range(1, NX):
                    x1_copy(k, j).wait_send()

    drains.append(drain_3)

    mine = onehot(iota((32, 512), 1), iota((32, 512), 0) + rep * 32)

    def x1_copy(k, j):
        to = lax.rem(x + j, NX)
        rows = pl.ds(pl.multiple_of(x * 16, 16), 16)
        return remote(xs1.at[k, to], gall.at[k, y, :, rows], s_x1.at[k, j - 1], r_x1.at[k, x], at_x(to))

    def x1_wait(k, j):
        src = lax.rem(x + j, NX)
        rows = pl.ds(pl.multiple_of(src * 16, 16), 16)
        remote(xs1.at[k, src], gall.at[k, y, :, rows], s_x1.at[k, 0], r_x1.at[k, src], at_x(src)).wait_recv()

    def regroup_slot(k):
        for j in range(1, NZ):
            src = lax.rem(z + j, NZ)
            remote(v1.at[k, 0], w1.at[k, src], s_z1.at[k, 0], r_z1.at[k, src], at_z(src)).wait_recv()
        xs1[k] = mm(perm2[...], w1[k].reshape(256, 128)).astype(BF).reshape(NX, 4, 16, 128)
        for j in (2, 1, 3):
            x1_copy(k, j).start()
        gall[k, y, :, pl.ds(pl.multiple_of(x * 16, 16), 16)] = xs1[k, x]

    def h_copy(k, dy, cc):
        to = lax.rem(y + dy, NY) * 2 + cc
        return remote(hsend.at[k, to], hrecv.at[k, y], s_h.at[k, dy, cc], r_h.at[k, y], (to, own))

    def h_wait(k, dy):
        t = lax.rem(y + dy, NY)
        remote(hsend.at[k, 0], hrecv.at[k, t], s_h.at[k, 0, 0], r_h.at[k, t], sib).wait_recv()

    def own_copy(k):
        ref = gall.at[k, y]
        return remote(ref, ref, s_own.at[k], r_own.at[k], sib)

    far_first = (4, 3, 5, 2, 6, 1, 7)

    def left_product(k):
        for j in range(1, NX):
            x1_wait(k, j)
        hsend[k] = mm(qlt[k], gall[k, y].reshape(256, 128)).astype(BF).reshape(16, 32, 128)
        for dy in far_first:
            for cc in range(2):
                h_copy(k, dy, cc).start()
        for cc in range(2):

            @pl.when(c != cc)
            def _():
                h_copy(k, 0, cc).start()

        hrecv[k, y] = hsend[k, rep]
        own_copy(k).start()

    def ag_part(k, t, s, d):
        return gall.at[k, t] if s < 3 else gall.at[k, t, pl.ds(d * 2, 2)]

    def ag_copy(d, s, k):
        sign = 1 - 2 * d
        ref = ag_part(k, lax.rem(y - sign * s + NY, NY), s, d)
        return remote(ref, ref, s_ag.at[d, s, k], r_ag.at[d, s, k], at_y(y + sign, c))

    def ag_arrival(d, s, k):
        return ag_part(k, lax.rem(y - (1 - 2 * d) * (s + 1) + NY, NY), s, d)

    def sib_copy(i, k):
        ref = ag_arrival(i // 4, i % 4, k)
        return remote(ref, ref, s_sib.at[i, k], r_sib.at[i, k], sib)

    def gather(s, ks):
        @pl.when(jnp.logical_not(active))
        def _():
            for k in ks:
                if s == 0:
                    own_copy(k).wait_recv()
                for d in range(2):
                    if s > 0:
                        ref = ag_arrival(d, s - 1, k)
                        remote(ref, ref, s_ag.at[d, s - 1, k], r_ag.at[d, s - 1, k], sib).wait_recv()
                    if s < 4:
                        ag_copy(d, s, k).start()
                if s > 0:
                    for d in range(2):
                        sib_copy(d * 4 + s - 1, k).start()

    @pl.when(active)
    def _():
        regroup_slot(0)
        regroup_slot(1)
        for k in range(SLOTS):
            if k + 2 < SLOTS:
                regroup_slot(k + 2)
            left_product(k)

    def out_copies(k):
        return [
            pltpu.make_async_copy(o1.at[k], out_1.at[k], s_out.at[0, k]),
            pltpu.make_async_copy(o2.at[k], out_2.at[k], s_out.at[1, k]),
            pltpu.make_async_copy(ol.at[k], out_l.at[k], s_out.at[2, k]),
            pltpu.make_async_copy(orr.at[k], out_r.at[k], s_out.at[3, k]),
        ]

    lane_low = iota((32, 128), 1) < 64
    back = {}

    def slot_products(k):
        for dy in range(1, NY):
            h_wait(k, dy)

        @pl.when(jnp.logical_not(active))
        def _():
            h_wait(k, 0)

        h = jnp.concatenate(
            [(hrecv[k, q].astype(F32) + hrecv[k, q + 4].astype(F32)).astype(BF) for q in range(4)], axis=1
        )
        rotated = mm(h, qr[k].reshape(512, 512))
        first = BETA_FIRST * m1[k] + (1.0 - BETA_FIRST) * rotated
        second = BETA_SECOND * m2[k] + (1.0 - BETA_SECOND) * rotated * rotated
        o1[k] = first
        o2[k] = second
        for copy in out_copies(k)[:2]:
            copy.start()
        direction = (first / (jnp.sqrt(second) + EPSILON)).astype(BF)
        if k in (0, 2, 4):
            back[k, 0] = mm_t(direction, qr[k].reshape(512, 512)).astype(BF)
        if k in (1, 3, 4):
            back[k, 1] = mm_t(direction, qrs[(k - 1) // 2 if k < 4 else 2].reshape(512, 512)).astype(BF)

    def b_copy(p, dy):
        yy = lax.rem(y + dy, NY)
        return remote(bmsg.at[p, yy], bb.at[p, rep], s_b.at[p, dy], r_b.at[p, rep], (yy * 2 + PAIR_CORE[p], own))

    def send_back(p):
        a, b = PAIRS[p]
        for yy in range(NY):
            lanes = slice((yy // 2) * 128, (yy // 2) * 128 + 128)
            lo, hi = back[a, 0][:, lanes], back[b, 1][:, lanes]
            bmsg[p, yy] = jnp.where(lane_low, lo, hi) if yy % 2 == 0 else jnp.where(lane_low, hi, lo)
        for dy in far_first:
            b_copy(p, dy).start()

        @pl.when(c != PAIR_CORE[p])
        def _():
            b_copy(p, 0).start()

        @pl.when(c == PAIR_CORE[p])
        def _():
            bb[p, rep] = bmsg[p, y]

    def stat_products(k):
        @pl.when(active)
        def _():
            for i in range(8):
                ref = ag_arrival(i // 4, i % 4, k)
                remote(ref, ref, s_sib.at[i, k], r_sib.at[i, k], sib).wait_recv()

        for t in range(NY):
            gf[pl.ds((t // 4) * 256, 256), pl.ds((t % 4) * 128, 128)] = gall[k, t].reshape(256, 128)
        columns = mm_t(mine, gf[...]).astype(BF)
        right = mm(columns, gf[...])
        orr[k] = (BETA_SECOND * sr[k].astype(F32) + (1.0 - BETA_SECOND) * right).astype(BF)
        rows = mm(pm[pl.ds(pl.multiple_of(rep * 32, 32), 32), :], gf[...]).astype(BF)
        left = mm_t(rows, gf[...])
        high = left.astype(BF)
        low = (left - high.astype(F32)).astype(BF)
        left = mm_t(high, pm[...]) + mm_t(low, pm[...])
        ol[k] = (BETA_SECOND * sl[k].astype(F32) + (1.0 - BETA_SECOND) * left).astype(BF)
        for copy in out_copies(k)[2:]:
            copy.start()

    def z2_copy(p, j):
        to = lax.rem(z + j, NZ)
        if p == 2:
            src, dst = ub4.at[to], w24.at[z]
        else:
            src, dst = ub.at[p, pl.ds(pl.multiple_of(to * 32, 32), 32)], w2.at[p, z]
        return remote(src, dst, s_z2.at[p, j - 1], r_z2.at[p, z], at_z(to))

    def z2_wait(p, j):
        src = lax.rem(z + j, NZ)
        a, b = (ub4.at[0], w24.at[src]) if p == 2 else (ub.at[p, pl.ds(0, 32)], w2.at[p, src])
        remote(a, b, s_z2.at[p, 0], r_z2.at[p, src], at_z(src)).wait_recv()

    def x2_copy(p, j):
        to = lax.rem(x + j, NX)
        part = lax.rem(to, 2) if p == 2 else to
        return remote(xs2.at[p, part], yb.at[p, x], s_x2.at[p, j - 1], r_x2.at[p, x], at_x(to))

    def y_copy(p):
        return remote(yb.at[p], yb.at[p], s_y.at[p], r_y.at[p], sib)

    def update_products(p):
        for d in range(1, 16):
            src = lax.rem(rep + d, 16)
            remote(bmsg.at[p, 0], bb.at[p, src], s_b.at[p, 0], r_b.at[p, src], (src, own)).wait_recv()
        a, b = PAIRS[p]
        columns = bb[p].reshape(512, 128)
        if p == 2:
            whole = mm(ql[a], columns).astype(BF).reshape(NZ, 2, 16, 128)
            low = iota((NZ, 16, 128), 2) < 64
            ub4[...] = jnp.where(low, whole[:, 0], whole[:, 1])
        else:
            swap = jnp.where(iota((512, 128), 1) < 64, 0, 1) == (y & 1)
            ub[p] = jnp.where(swap, mm(ql[a], columns), mm(ql[b], columns)).astype(BF)
        for j in (8, 7, 9, 6, 10, 5, 11, 4, 12, 3, 13, 2, 14, 1, 15):
            z2_copy(p, j).start()
        if p == 2:
            w24[z] = ub4[z]
        else:
            w2[p, z] = ub[p, pl.ds(pl.multiple_of(z * 32, 32), 32)]

    def update_regroup(p):
        for j in range(1, NZ):
            z2_wait(p, j)
        if p == 2:
            parts = mm(perm4[...], w24[...].reshape(256, 128)).astype(BF).reshape(2, 8, 16, 128)
            xs2[p, pl.ds(0, 2)] = parts
        else:
            xs2[p] = mm(perm3[...], w2[p].reshape(512, 128)).astype(BF).reshape(NX, 8, 16, 128)
        for j in (2, 1, 3):
            x2_copy(p, j).start()
        yb[p, x] = xs2[p, lax.rem(x, 2) if p == 2 else x]

    def update_share(p):
        for j in range(1, NX):
            src = lax.rem(x + j, NX)
            remote(xs2.at[p, 0], yb.at[p, src], s_x2.at[p, 0], r_x2.at[p, src], at_x(src)).wait_recv()
        y_copy(p).start()

    slot_products(0)
    gather(0, (0, 1, 2))
    slot_products(1)
    send_back(0)
    gather(0, (3, 4))
    slot_products(2)
    slot_products(3)
    send_back(1)
    gather(1, (0, 1))
    slot_products(4)
    send_back(2)
    gather(1, (2, 3, 4))
    j3 = iota((512, 1), 0)
    perm3[...] = onehot(iota((512, 512), 1), (j3 & 15) * 32 + (j3 >> 7) * 8 + ((j3 >> 4) & 7))
    perm4[...] = onehot(iota((256, 256), 1), (j2 & 15) * 16 + (j2 >> 7) * 8 + ((j2 >> 4) & 7))
    oh2[...] = onehot(iota((512, PADB), 0), slot_code)
    yb[pl.ds(3, 1)] = jnp.zeros((1, NX, 8, 16, 128), BF)

    def on_core(core, steps):
        @pl.when(c == core)
        def _():
            for step, p in steps:
                step(p)

    on_core(0, [(update_products, 0)])
    gather(2, (0, 1, 2, 3, 4))
    on_core(0, [(update_products, 2), (update_regroup, 0)])
    on_core(1, [(update_products, 1)])
    gather(3, (0, 1, 2, 3, 4))
    on_core(0, [(update_share, 0)])
    on_core(1, [(update_regroup, 1)])
    gather(4, (0, 1))
    stat_products(0)
    stat_products(1)
    gather(4, (2, 3, 4))
    on_core(0, [(update_regroup, 2)])
    on_core(1, [(update_share, 1)])
    stat_products(2)
    stat_products(3)
    on_core(0, [(update_share, 2)])
    stat_products(4)

    @pl.when(c == 0)
    def _():
        y_copy(1).wait_recv()

    @pl.when(c == 1)
    def _():
        y_copy(0).wait_recv()
        y_copy(2).wait_recv()

    chosen = onehot(
        iota((64, 128), 1), (iota((64, 1), 0) >> 5) * 64 + 32 * c + (iota((64, 1), 0) & 31)
    )
    for i in range(8):
        lanes = mm_t(chosen, yb[:, :, i].reshape(256, 128)).astype(BF)
        wbuf[pl.ds(i * 32, 32), pl.ds(0, 256)] = lanes[:32]
        wbuf[pl.ds(i * 32, 32), pl.ds(256, 256)] = lanes[32:]
    out_u[...] = mm(wbuf[...], oh2[...]).astype(BF)[:, :NB]

    def drain_4():
        @pl.when(active)
        def _():
            for k in range(SLOTS):
                for dy in far_first:
                    for cc in range(2):
                        h_copy(k, dy, cc).wait_send()
                for cc in range(2):

                    @pl.when(c != cc)
                    def _():
                        h_copy(k, 0, cc).wait_send()

                own_copy(k).wait_send()

        @pl.when(jnp.logical_not(active))
        def _():
            for k in range(SLOTS):
                for s in range(4):
                    for d in range(2):
                        ag_copy(d, s, k).wait_send()
                        sib_copy(d * 4 + s, k).wait_send()

        for p in range(3):
            for dy in far_first:
                b_copy(p, dy).wait_send()

            @pl.when(c != PAIR_CORE[p])
            def _():
                b_copy(p, 0).wait_send()

            @pl.when(c == PAIR_CORE[p])
            def _():
                for j in range(1, NZ):
                    z2_copy(p, j).wait_send()
                for j in range(1, NX):
                    x2_copy(p, j).wait_send()
                y_copy(p).wait_send()

    drains.append(drain_4)
    for k in range(SLOTS):
        for copy in out_copies(k):
            copy.wait()
    for drain in drains:
        drain()


def onehot_lt(a, b):
    return jnp.where(a < b, 1.0, 0.0).astype(BF)


def hand_on(*refs):
    count = len(refs) // 2
    for i in range(count):
        refs[count + i][...] = refs[i][...]


def shards(grad_parts, owner_of, stats_left, stats_right, basis_left, basis_right, moment_first, moment_second):
    blocks = owner_of.shape[0]
    padded = jnp.pad(owner_of[:, 0], (0, PADB - blocks), constant_values=-1)
    anywhere = pl.BlockSpec(memory_space=pl.ANY)
    vmem = pl.BlockSpec(memory_space=pltpu.VMEM)
    rows = (SLOTS, 32, 512)
    dma = pltpu.SemaphoreType.DMA
    scratch = [
        pltpu.VMEM((1152, 256), BF),
        pltpu.VMEM((1152, 256), BF),
        pltpu.VMEM((4, NB, 512), BF),
        pltpu.VMEM((2, 4, NB, 512), BF),
        pltpu.VMEM((2, 3, NB, 512), BF),
        pltpu.VMEM((PADB, 512), BF),
        pltpu.VMEM((4, 640, PADB), BF),
        pltpu.VMEM((SLOTS, 8, 16, 128), BF),
        pltpu.VMEM((SLOTS, NZ, 16, 128), BF),
        pltpu.VMEM((SLOTS, NX, 4, 16, 128), BF),
        pltpu.VMEM((SLOTS, NY, 4, 64, 128), BF),
        pltpu.VMEM((SLOTS, 512, 512), BF),
        pltpu.VMEM((SLOTS, 4, 2, 64, 512), BF),
        pltpu.VMEM((3, 4, 2, 64, 512), BF),
        pltpu.VMEM(rows, BF),
        pltpu.VMEM(rows, BF),
        pltpu.VMEM(rows, F32),
        pltpu.VMEM(rows, F32),
        pltpu.VMEM(rows, BF),
        pltpu.VMEM(rows, BF),
        pltpu.VMEM(rows, F32),
        pltpu.VMEM(rows, F32),
        pltpu.VMEM((SLOTS, 512, 256), BF),
        pltpu.VMEM((SLOTS, 16, 32, 128), BF),
        pltpu.VMEM((SLOTS, NY, 32, 128), BF),
        pltpu.VMEM((512, 512), BF),
        pltpu.VMEM((512, 512), BF),
        pltpu.VMEM((256, 256), BF),
        pltpu.VMEM((512, 512), BF),
        pltpu.VMEM((256, 256), BF),
        pltpu.VMEM((512, PADB), BF),
        pltpu.VMEM((256, 512), BF),
        pltpu.VMEM((3, NY, 32, 128), BF),
        pltpu.VMEM((3, 16, 32, 128), BF),
        pltpu.VMEM((2, 512, 128), BF),
        pltpu.VMEM((NZ, 16, 128), BF),
        pltpu.VMEM((2, NZ, 32, 128), BF),
        pltpu.VMEM((NZ, 16, 128), BF),
        pltpu.VMEM((3, NX, 8, 16, 128), BF),
        pltpu.VMEM((4, NX, 8, 16, 128), BF),
        dma((13,)),
        dma((4, SLOTS)),
        dma((3,)), dma((3,)),
        dma((2, 4, SUBS)), dma((2, 4, SUBS)),
        dma((SUBS,)), dma((SUBS,)),
        dma((SLOTS, 8)), dma((SLOTS, NZ)),
        dma((SLOTS, 3)), dma((SLOTS, NX)),
        dma((SLOTS, NY, 2)), dma((SLOTS, NY)),
        dma((SLOTS,)), dma((SLOTS,)),
        dma((2, 4, SLOTS)), dma((2, 4, SLOTS)),
        dma((8, SLOTS)), dma((8, SLOTS)),
        dma((3, NY)), dma((3, 16)),
        dma((3, NZ - 1)), dma((3, NZ)),
        dma((3, NX - 1)), dma((3, NX)),
        dma((3,)), dma((3,)),
    ]
    shapes = (
        jax.ShapeDtypeStruct(rows, BF),
        jax.ShapeDtypeStruct(rows, BF),
        jax.ShapeDtypeStruct(rows, F32),
        jax.ShapeDtypeStruct(rows, F32),
        jax.ShapeDtypeStruct((256, blocks), BF),
    )
    results = pl.pallas_call(
        kernel,
        out_shape=shapes,
        in_specs=[anywhere, vmem] + [anywhere] * 6,
        out_specs=(anywhere,) * 4 + (vmem,),
        scratch_shapes=scratch,
        compiler_params=pltpu.CompilerParams(
            collective_id=0, has_side_effects=True, vmem_limit_bytes=56 * 1024 * 1024
        ),
    )(
        grad_parts[0].reshape(blocks * 8, 512),
        padded[None, :],
        stats_left[0],
        stats_right[0],
        basis_left[0],
        basis_right[0].reshape(SLOTS, 4, 2, 64, 512),
        moment_first[0],
        moment_second[0],
    )
    new_left, new_right, new_first, new_second, picked = pl.pallas_call(
        hand_on,
        out_shape=shapes,
        in_specs=[vmem] * 5,
        out_specs=(vmem,) * 5,
    )(*results)
    update = picked.reshape(8, 32, blocks).transpose(2, 0, 1)
    return (new_left[None], new_right[None], new_first[None], new_second[None], update)


def solution(mesh):
    return jax.shard_map(
        shards,
        mesh=mesh,
        in_specs=(
            P("replica", None, "owner", None),
            P(),
            P("owner", None, "replica", None),
            P("owner", None, "replica", None),
            P("owner", None, None, None),
            P("owner", None, None, None),
            P("owner", None, "replica", None),
            P("owner", None, "replica", None),
        ),
        out_specs=(
            P("owner", None, "replica", None),
            P("owner", None, "replica", None),
            P("owner", None, "replica", None),
            P("owner", None, "replica", None),
            P(None, "owner", "replica"),
        ),
        check_vma=False,
    )
```

time: 270 us -> 102 us (0.38)
  waiting for transfers between devices: 181 us -> 0 us
  Pallas kernels: 0 us -> 100 us
  blocking collectives: 30.9 us -> 0 us
  starting transfers between devices: 16.2 us -> 0 us
  matrix products: 14.4 us -> 0 us
  between operations: 13.9 us -> 0.64 us
  local copies, waits for them, and re-layouts: 11.3 us -> 1.24 us
    pallas_call x0 -> x2, Pallas kernels: none -> 100 us  [the longest x1 97.8 us: shards(): pl.pallas_call(kernel, out_shape=shapes, in_specs=[anywhere, vmem] + [any...]
    all_gather x2 -> x0, waiting for transfers between devices: 91.3 us -> none  [the longest x1 47.3 us: shards(): all_rows = lax.all_gather(direction, 'replica', axis=1, tiled=True)]
    reduce_scatter x1 -> x0, waiting for transfers between devices: 74.3 us -> none  [shards(): lax.psum_scatter(grad_parts[0].astype(jnp.float32).astype(jnp.bfloat16),...]
    all_to_all x1 -> x0, blocking collectives: 30.9 us -> none  [shards(): lax.all_to_all(outgoing, 'owner', split_axis=1, concat_axis=1, tiled=True)]
    all_to_all x1 -> x0, starting transfers between devices: 16.1 us -> none  [shards(): lax.all_to_all(leaving, 'owner', split_axis=1, concat_axis=1, tiled=True)]
    all_to_all x1 -> x0, waiting for transfers between devices: 15.2 us -> none  [shards(): lax.all_to_all(leaving, 'owner', split_axis=1, concat_axis=1, tiled=True)]
    dot_general x6 -> x0, matrix products: 14.4 us -> none  [the longest x1 4.65 us: shards(): jnp.einsum('sic,scj->sij', half_rot, right_basis, preferred_element_type=...]
    unnamed x9 -> x0, local copies, waits for them, and re-layouts: 4.66 us -> none
  transfers between devices with their start and end apart: 4 -> 0, of which waited for: 4 -> 0; matrix products, arithmetic and copies ran while one was open for 2% -> 0% of each run, Pallas kernels for 0% -> 0%
where the time goes in v2:
time: 102 us
  Pallas kernels  100 us (98%)
  local copies, waits for them, and re-layouts  1.24 us (1%)
    pallas_call x1, Pallas kernels, shards(): pl.pallas_call(kernel, out_shape=shapes, in_specs=[anywhere, vmem] + [any...  97.8 us
    pallas_call x1, Pallas kernels, shards(): pl.pallas_call(hand_on, out_shape=shapes, in_specs=[vmem] * 5, out_specs=...  2.26 us

profile of v2, /device:TPU:1, one launch (start us, length us, event | category | flops | bytes accessed | tf_op | source)
XLA Modules:
  0.0 102.0 jit_solution(1028939027804553482)
XLA Ops:
  0.6 1.2 %pad.4 = s32[256]{0:T(256)} pad(s32[144]{0:T(256)} %bitcast.24, s32[]{:T(128)} %constant.0.clone.1), padding=0_112 | pad | bytes 1604 | tf_op jit(solution)/shard_map/jit(_pad)/pad | solution.py:629
  1.9 97.8 %shard_map.119 = (bf16[5,32,512]{2,1,0:T(8,128)(2,1)}, bf16[5,32,512]{2,1,0:T(8,128)(2,1)}, f32[5,32,512]{2,1,0:T(8,128)}, f32[5,32,512]{2,1,0:T(8,128)}, bf16[256,144]{1,0:T(8,128)(2,1)}) custom-call(bf16[1152,512]{1,0:T(8,128)(2,1)} %bitcast.18, s32[1,256]{1,0:T(1,128)} %bitcast.23, bf16[5,32,512]{2,1,0:T(8,128)(2,1)} %bitcast.21, ...), custom_call_target="tpu_custom_call" | custom-call | tf_op jit(solution)/shard_map/pallas_call | solution.py:698
  99.7 2.3 %shard_map.120 = (bf16[5,32,512]{2,1,0:T(8,128)(2,1)}, bf16[5,32,512]{2,1,0:T(8,128)(2,1)}, f32[5,32,512]{2,1,0:T(8,128)}, f32[5,32,512]{2,1,0:T(8,128)}, bf16[256,144]{1,0:T(8,128)(2,1)}) custom-call(bf16[5,32,512]{2,1,0:T(8,128)(2,1)} %get-tuple-element.15.refs_0_, bf16[5,32,512]{2,1,0:T(8,128)(2,1)} %get-tuple-element.16.refs_1_, ...), custom_call_target="tpu_custom_call" | custom-call | tf_op jit(solution)/shard_map/pallas_call | solution.py:717

commit v3 on v2

v3 whole, which is shorter than its diff:
```python
import jax
import jax.numpy as jnp
from jax import lax
from jax.experimental import pallas as pl
from jax.experimental.pallas import tpu as pltpu
from jax.sharding import PartitionSpec as P

BETA_FIRST = 0.9
BETA_SECOND = 0.95
EPSILON = 1e-08
MESH = pl.DeviceIdType.MESH
BF = jnp.bfloat16
F32 = jnp.float32
NY, NX, NZ = 8, 4, 16
NB, PADB = 144, 256
SLOTS = 5
SUBS, SUBROWS = 3, 48
PAIRS = ((0, 1), (2, 3), (4, 4))
PAIR_CORE = (0, 1, 0)


def mm(a, b):
    return jnp.dot(a, b, preferred_element_type=F32)


def mm_t(a, b):
    return lax.dot_general(a, b, (((1,), (1,)), ((), ())), preferred_element_type=F32)


def iota(shape, axis):
    return lax.broadcasted_iota(jnp.int32, shape, axis)


def onehot(a, b):
    return jnp.where(a == b, 1.0, 0.0).astype(BF)


def kernel(
    grad, own_row, stats_l, stats_r, basis_l, basis_r, mom1, mom2,
    out_l, out_r, out_1, out_2, out_u,
    go, gx, chunk, rs_mid, rs_end, rs_send, summed, place, v1, w1, xs1, gall,
    ql, qr, qrs, sl, sr, m1, m2, ol, orr, o1, o2, qlt, hsend, hrecv, gf, pm, perm2, perm3, perm4, oh2, wbuf,
    bmsg, bb, ub, ub4, w2, w24, xs2, yb,
    s_in, s_out, s_core, r_core, s_rs, r_mid, r_end, s_cag, r_cag, s_z1, r_z1, s_x1, r_x1,
    s_h, r_h, s_own, r_own, s_ag, r_ag, s_sib, r_sib, s_b, r_b, s_z2, r_z2, s_x2, r_x2, s_y, r_y,
):
    rep = lax.axis_index("replica")
    own = lax.axis_index("owner")
    y, c = rep // 2, rep % 2
    z, x = own // NX, own % NX
    sib = (y * 2 + (1 - c), own)
    zhalf = z // 8
    active = c == zhalf

    def at_y(yy, cc):
        return (lax.rem(yy + 2 * NY, NY) * 2 + cc, own)

    def at_z(zz):
        return (rep, zz * NX + x)

    def at_x(xx):
        return (rep, z * NX + xx)

    def remote(src, dst, ssem, rsem, dev):
        return pltpu.make_async_remote_copy(
            src_ref=src, dst_ref=dst, send_sem=ssem, recv_sem=rsem, device_id=dev, device_id_type=MESH
        )

    def received(ref, sem):
        remote(ref, ref, sem, sem, sib).wait_recv()

    def sent(ref, sem):
        remote(ref, ref, sem, sem, sib).wait_send()

    half = pl.ds(pl.multiple_of(c * 256, 256), 256)
    other = pl.ds(pl.multiple_of((1 - c) * 256, 256), 256)
    loads = [pltpu.make_async_copy(grad.at[:, half], go, s_in.at[0])]
    loads += [
        pltpu.make_async_copy(src, dst, s_in.at[1 + i])
        for i, (src, dst) in enumerate(
            ((basis_l, ql), (basis_r, qr), (stats_l, sl), (stats_r, sr), (mom1, m1), (mom2, m2))
        )
    ]
    swaps = [
        pltpu.make_async_copy(basis_r.at[k, :, h], qrs.at[i, :, 1 - h], s_in.at[7])
        for i, k in enumerate((1, 3, 4))
        for h in range(2)
    ]
    loads[0].start()
    drains = []

    barrier = pltpu.get_barrier_semaphore()
    for d in range(1, 16):
        pl.semaphore_signal(barrier, inc=1, device_id=(lax.rem(rep + d, 16), own), device_id_type=MESH)
    for d in range(1, NZ):
        pl.semaphore_signal(barrier, inc=1, device_id=at_z(lax.rem(z + d, NZ)), device_id_type=MESH)
    for d in range(1, NX):
        for cc in range(2):
            to = (y * 2 + cc, z * NX + lax.rem(x + d, NX))
            pl.semaphore_signal(barrier, inc=1, device_id=to, device_id_type=MESH)
    pl.semaphore_wait(barrier, 15 + NZ - 1 + 2 * (NX - 1))

    def core_copy(j):
        rows = pl.ds(j * 384, 384)
        return remote(grad.at[rows, other], gx.at[rows], s_core.at[0], r_core.at[j], sib)

    def rs_target(step):
        t = lax.rem(y + step + NY, NY)
        return (t // 4) * 2 + t % 2, c == (t % 4) // 2

    def rs_copy(d, step, j):
        sign = 1 - 2 * d
        rows = pl.ds(j * SUBROWS, SUBROWS)
        which = rs_target(sign * step)[0]
        if step == 4:
            lanes = pl.ds(d * 256, 256)
            src, dst = chunk.at[which, rows, lanes], rs_mid.at[d, 0, rows, lanes]
            sem, to = r_mid.at[d, 0, j], y + 2 * sign
        elif step == 3:
            src, dst = chunk.at[which, rows], rs_mid.at[d, 1, rows]
            sem, to = r_mid.at[d, 1, j], y + sign
        elif step == 2:
            src, dst = rs_send.at[d, rows], rs_end.at[d, 1, rows]
            sem, to = r_end.at[j], y + 2 * sign
        else:
            src, dst = chunk.at[which, rows], rs_end.at[d, 0, rows]
            sem, to = r_end.at[j], y + sign
        return remote(src, dst, s_rs.at[0], sem, at_y(to, c))

    def rs_start(step, j):
        for d in range(2):

            @pl.when(rs_target((1 - 2 * d) * step)[1])
            def _():
                rs_copy(d, step, j).start()

    for j in range(3):
        core_copy(j).start()
    for d in loads[1:] + swaps:
        d.start()

    out_of = iota((128, 1), 0)
    perm1 = onehot(iota((128, 128), 1), (out_of % 16) * 8 + out_of // 16)
    o_row = own_row[...]
    e_row = onehot(iota((128, PADB), 0), o_row)
    before = mm(e_row, onehot_lt(iota((PADB, PADB), 0), iota((PADB, PADB), 1)))
    k_row = jnp.sum(before * e_row.astype(F32), axis=0, keepdims=True).astype(jnp.int32)
    zr, xr = o_row >> 2, o_row & 3
    code = jnp.where((zr >> 3) == c, (k_row * 8 + (zr & 7)) * 16 + xr, -64)
    for q in range(4):
        place[q] = onehot(iota((640, PADB), 0), code + 4 * q)
    side = jnp.where(k_row == 4, x >> 1, (k_row + y) & 1)
    slot_code = side * 256 + (k_row >> 1) * 64 + xr * 16 + zr
    summed[pl.ds(NB, PADB - NB), :] = jnp.zeros((PADB - NB, 512), BF)

    loads[0].wait()
    for j in range(3):
        core_copy(j).wait_recv()
        for g in range(3 * j, 3 * j + 3):
            rows = pl.ds(g * 128, 128)
            both = (mm(perm1, go[rows, :]) + mm(perm1, gx[rows, :])).astype(BF)
            for i in range(8):
                for q in range(2):
                    chunk[(i // 4) * 2 + q, pl.ds(g * 16, 16), pl.ds((i % 4) * 128, 128)] = both[
                        i * 16 : i * 16 + 16, q * 128 : q * 128 + 128
                    ]

        rs_start(4, j)
        rs_start(3, j)
    drains.append(lambda: sent(gx, s_core.at[0]))
    for j in range(SUBS):
        rs_start(1, j)

    for d in loads[1:]:
        d.wait()
    pltpu.make_async_copy(qrs, qrs, s_in.at[7]).wait()
    r_col = iota((256, 1), 0)
    held = ((r_col & 15) * 4 + ((r_col >> 4) & 3)) * 8 + (y // 4) * 4 + (r_col >> 6)
    held_rows = onehot(iota((256, 512), 1), held)
    same = onehot(iota((512, 512), 0), iota((512, 512), 1))

    def turn_basis(k):
        qlt[k] = mm_t(same, mm(held_rows, ql[k]).astype(BF)).astype(BF)

    turn_basis(0)
    turn_basis(1)
    turn_basis(2)

    for j in range(SUBS):
        for d in range(2):
            rows = pl.ds(j * SUBROWS, SUBROWS)
            t, here = rs_target((1 - 2 * d) * 2)

            @pl.when(here)
            def _():
                lanes = pl.ds(d * 256, 256)
                rest = pl.ds((1 - d) * 256, 256)
                received(rs_mid.at[d, 0, rows, lanes], r_mid.at[d, 0, j])
                received(rs_mid.at[d, 1, rows], r_mid.at[d, 1, j])
                rs_send[d, rows, lanes] = (
                    chunk[t, rows, lanes].astype(F32)
                    + rs_mid[d, 0, rows, lanes].astype(F32)
                    + rs_mid[d, 1, rows, lanes].astype(F32)
                ).astype(BF)
                rs_send[d, rows, rest] = (
                    chunk[t, rows, rest].astype(F32) + rs_mid[d, 1, rows, rest].astype(F32)
                ).astype(BF)
                rs_copy(d, 2, j).start()

    turn_basis(3)
    turn_basis(4)
    j2 = iota((256, 1), 0)
    perm2[...] = onehot(iota((256, 256), 1), (j2 & 15) * 16 + ((j2 >> 4) & 3) * 4 + (j2 >> 6))
    rho = iota((1, 512), 1)
    natural = ((rho & 15) * 4 + ((rho >> 4) & 3)) * 8 + (rho >> 8) * 4 + ((rho >> 6) & 3)
    pm[...] = onehot(iota((512, 512), 0), natural)
    last, sums_here = rs_target(0)
    sums = summed.at[pl.ds(0, NB)]

    @pl.when(sums_here)
    def _():
        for j in range(SUBS):
            rows = pl.ds(j * SUBROWS, SUBROWS)
            received(rs_end.at[:, :, rows], r_end.at[j])
            total = chunk[last, rows].astype(F32)
            for d in range(2):
                total += rs_end[d, 0, rows].astype(F32) + rs_end[d, 1, rows].astype(F32)
            summed[rows] = total.astype(BF)
            ref = summed.at[rows]
            remote(ref, ref, s_cag.at[0], r_cag.at[0], sib).start()

    @pl.when(jnp.logical_not(sums_here))
    def _():
        received(sums, r_cag.at[0])

    def drain_2():
        @pl.when(sums_here)
        def _():
            sent(chunk.at[pl.ds(0, 3)], s_rs.at[0])
            sent(sums, s_cag.at[0])

        @pl.when(jnp.logical_not(sums_here))
        def _():
            sent(chunk, s_rs.at[0])

    drains.append(drain_2)

    def z1_copy(k, j):
        low = lax.rem(z + j + 4 * active.astype(jnp.int32), 8)
        return remote(v1.at[k, low], w1.at[k, z], s_z1.at[0], r_z1.at[k], at_z(c * 8 + low))

    def fill_slots(k, n):
        rows = pl.ds(k * 128, n * 128)
        placed = mm(place[0, rows], summed[:, pl.ds(0, 128)])
        for q in range(1, 4):
            placed += mm(place[q, rows], summed[:, pl.ds(q * 128, 128)])
        v1[pl.ds(k, n)] = placed.astype(BF).reshape(n, 8, 16, 128)
        for kk in range(k, k + n):
            for j in (0, 1, 7, 2, 6, 3, 5):
                z1_copy(kk, j).start()

            @pl.when(jnp.logical_not(active))
            def _():
                z1_copy(kk, 4).start()

        @pl.when(active)
        def _():
            w1[pl.ds(k, n), z] = v1[pl.ds(k, n), lax.rem(z, 8)]

    fill_slots(0, 1)
    fill_slots(1, 4)

    def drain_3():
        @pl.when(jnp.logical_not(active))
        def _():
            sent(v1, s_z1.at[0])

        @pl.when(active)
        def _():
            sent(v1.at[:, pl.ds(0, 7)], s_z1.at[0])
            sent(xs1.at[:, pl.ds(0, NX - 1)], s_x1.at[0])

    drains.append(drain_3)

    mine = onehot(iota((32, 512), 1), iota((32, 512), 0) + rep * 32)

    def x1_copy(k, j):
        to = lax.rem(x + j, NX)
        rows = pl.ds(pl.multiple_of(x * 16, 16), 16)
        return remote(xs1.at[k, to], gall.at[k, y, :, rows], s_x1.at[0], r_x1.at[k], at_x(to))

    def regroup_slot(k):
        received(w1.at[k, pl.ds(0, NZ - 1)], r_z1.at[k])
        xs1[k] = mm(perm2[...], w1[k].reshape(256, 128)).astype(BF).reshape(NX, 4, 16, 128)
        for j in (2, 1, 3):
            x1_copy(k, j).start()
        gall[k, y, :, pl.ds(pl.multiple_of(x * 16, 16), 16)] = xs1[k, x]

    def h_copy(k, dy, cc):
        to = lax.rem(y + dy, NY) * 2 + cc
        return remote(hsend.at[k, to], hrecv.at[k, y], s_h.at[0], r_h.at[k], (to, own))

    def own_copy(k):
        ref = gall.at[k, y]
        return remote(ref, ref, s_own.at[0], r_own.at[k], sib)

    far_first = (4, 3, 5, 2, 6, 1, 7)

    def left_product(k):
        received(xs1.at[k, pl.ds(0, NX - 1)], r_x1.at[k])
        hsend[k] = mm(qlt[k], gall[k, y].reshape(256, 128)).astype(BF).reshape(16, 32, 128)
        for dy in far_first:
            for cc in range(2):
                h_copy(k, dy, cc).start()
        for cc in range(2):

            @pl.when(c != cc)
            def _():
                h_copy(k, 0, cc).start()

        hrecv[k, y] = hsend[k, rep]
        own_copy(k).start()

    groups = ((0, 2), (2, 3))

    def ag_part(g, t, s, d):
        ks = pl.ds(*groups[g])
        return gall.at[ks, t] if s < 3 else gall.at[ks, t, pl.ds(d * 2, 2)]

    def ag_copy(d, s, g):
        sign = 1 - 2 * d
        ref = ag_part(g, lax.rem(y - sign * s + NY, NY), s, d)
        return remote(ref, ref, s_ag.at[0], r_ag.at[d, s, g], at_y(y + sign, c))

    def ag_arrival(d, s, g):
        return ag_part(g, lax.rem(y - (1 - 2 * d) * (s + 1) + NY, NY), s, d)

    def gather(s, g):
        @pl.when(jnp.logical_not(active))
        def _():
            if s == 0:
                for k in range(groups[g][0], sum(groups[g])):
                    received(gall.at[k, y], r_own.at[k])
            for d in range(2):
                if s > 0:
                    received(ag_arrival(d, s - 1, g), r_ag.at[d, s - 1, g])
                if s < 4:
                    ag_copy(d, s, g).start()
            if s > 0:
                for d in range(2):
                    ref = ag_arrival(d, s - 1, g)
                    remote(ref, ref, s_sib.at[0], r_sib.at[g], sib).start()

    @pl.when(active)
    def _():
        regroup_slot(0)
        regroup_slot(1)
        for k in range(SLOTS):
            if k + 2 < SLOTS:
                regroup_slot(k + 2)
            left_product(k)

    def out_copies(k):
        return [
            pltpu.make_async_copy(src.at[k], dst.at[k], s_out.at[i])
            for i, (src, dst) in enumerate(((o1, out_1), (o2, out_2), (ol, out_l), (orr, out_r)))
        ]

    lane_low = iota((32, 128), 1) < 64
    back = {}

    def slot_products(k):
        @pl.when(active)
        def _():
            received(hrecv.at[k, pl.ds(0, NY - 1)], r_h.at[k])

        @pl.when(jnp.logical_not(active))
        def _():
            received(hrecv.at[k], r_h.at[k])

        h = jnp.concatenate(
            [(hrecv[k, q].astype(F32) + hrecv[k, q + 4].astype(F32)).astype(BF) for q in range(4)], axis=1
        )
        rotated = mm(h, qr[k].reshape(512, 512))
        first = BETA_FIRST * m1[k] + (1.0 - BETA_FIRST) * rotated
        second = BETA_SECOND * m2[k] + (1.0 - BETA_SECOND) * rotated * rotated
        o1[k] = first
        o2[k] = second
        for copy in out_copies(k)[:2]:
            copy.start()
        direction = (first / (jnp.sqrt(second) + EPSILON)).astype(BF)
        if k in (0, 2, 4):
            back[k, 0] = mm_t(direction, qr[k].reshape(512, 512)).astype(BF)
        if k in (1, 3, 4):
            back[k, 1] = mm_t(direction, qrs[(k - 1) // 2 if k < 4 else 2].reshape(512, 512)).astype(BF)

    def b_copy(p, dy):
        yy = lax.rem(y + dy, NY)
        return remote(bmsg.at[p, yy], bb.at[p, rep], s_b.at[p], r_b.at[p], (yy * 2 + PAIR_CORE[p], own))

    def send_back(p):
        a, b = PAIRS[p]
        for yy in range(NY):
            lanes = slice((yy // 2) * 128, (yy // 2) * 128 + 128)
            lo, hi = back[a, 0][:, lanes], back[b, 1][:, lanes]
            bmsg[p, yy] = jnp.where(lane_low, lo, hi) if yy % 2 == 0 else jnp.where(lane_low, hi, lo)
        for dy in far_first:
            b_copy(p, dy).start()

        @pl.when(c != PAIR_CORE[p])
        def _():
            b_copy(p, 0).start()

        @pl.when(c == PAIR_CORE[p])
        def _():
            bb[p, rep] = bmsg[p, y]

    def stat_products(k):
        for g in range(2):
            if k == groups[g][0]:

                @pl.when(active)
                def _():
                    received(gall.at[pl.ds(*groups[g]), pl.ds(0, NY - 1)], r_sib.at[g])

        for t in range(NY):
            gf[pl.ds((t // 4) * 256, 256), pl.ds((t % 4) * 128, 128)] = gall[k, t].reshape(256, 128)
        columns = mm_t(mine, gf[...]).astype(BF)
        right = mm(columns, gf[...])
        orr[k] = (BETA_SECOND * sr[k].astype(F32) + (1.0 - BETA_SECOND) * right).astype(BF)
        rows = mm(pm[pl.ds(pl.multiple_of(rep * 32, 32), 32), :], gf[...]).astype(BF)
        left = mm_t(rows, gf[...])
        high = left.astype(BF)
        low = (left - high.astype(F32)).astype(BF)
        left = mm_t(high, pm[...]) + mm_t(low, pm[...])
        ol[k] = (BETA_SECOND * sl[k].astype(F32) + (1.0 - BETA_SECOND) * left).astype(BF)
        for copy in out_copies(k)[2:]:
            copy.start()

    def z2_copy(p, j):
        to = lax.rem(z + j, NZ)
        if p == 2:
            src, dst = ub4.at[to], w24.at[z]
        else:
            src, dst = ub.at[p, pl.ds(pl.multiple_of(to * 32, 32), 32)], w2.at[p, z]
        return remote(src, dst, s_z2.at[p], r_z2.at[p], at_z(to))

    def x2_copy(p, j, cc):
        to = lax.rem(x + j, NX)
        part = lax.rem(to, 2) if p == 2 else to
        return remote(xs2.at[p, part], yb.at[p, x], s_x2.at[p], r_x2.at[p], (y * 2 + cc, z * NX + to))

    def y_copy(p):
        return remote(yb.at[p], yb.at[p], s_y.at[p], r_y.at[p], sib)

    def update_products(p):
        received(bb.at[p, pl.ds(0, 15)], r_b.at[p])
        a, b = PAIRS[p]
        columns = bb[p].reshape(512, 128)
        if p == 2:
            whole = mm(ql[a], columns).astype(BF).reshape(NZ, 2, 16, 128)
            low = iota((NZ, 16, 128), 2) < 64
            ub4[...] = jnp.where(low, whole[:, 0], whole[:, 1])
        else:
            swap = jnp.where(iota((512, 128), 1) < 64, 0, 1) == (y & 1)
            ub[p] = jnp.where(swap, mm(ql[a], columns), mm(ql[b], columns)).astype(BF)
        for j in (8, 7, 9, 6, 10, 5, 11, 4, 12, 3, 13, 2, 14, 1, 15):
            z2_copy(p, j).start()
        if p == 2:
            w24[z] = ub4[z]
        else:
            w2[p, z] = ub[p, pl.ds(pl.multiple_of(z * 32, 32), 32)]

    def update_regroup(p):
        if p == 2:
            received(w24.at[pl.ds(0, NZ - 1)], r_z2.at[p])
            parts = mm(perm4[...], w24[...].reshape(256, 128)).astype(BF).reshape(2, 8, 16, 128)
            xs2[p, pl.ds(0, 2)] = parts
            for j in (2, 1, 3, 0):
                for cc in (1, 0)[: 1 + (j > 0)]:
                    x2_copy(p, j, cc).start()
            yb[p, x] = xs2[p, lax.rem(x, 2)]
        else:
            received(w2.at[p, pl.ds(0, NZ - 1)], r_z2.at[p])
            xs2[p] = mm(perm3[...], w2[p].reshape(512, 128)).astype(BF).reshape(NX, 8, 16, 128)
            for j in (2, 1, 3):
                x2_copy(p, j, PAIR_CORE[p]).start()
            yb[p, x] = xs2[p, x]

    def update_share(p):
        received(yb.at[p, pl.ds(0, NX - 1)], r_x2.at[p])
        if p != 2:
            y_copy(p).start()

    slot_products(0)
    gather(0, 0)
    slot_products(1)
    send_back(0)
    slot_products(2)
    gather(0, 1)
    slot_products(3)
    send_back(1)
    gather(1, 0)
    slot_products(4)
    send_back(2)
    j3 = iota((512, 1), 0)
    perm3[...] = onehot(iota((512, 512), 1), (j3 & 15) * 32 + (j3 >> 7) * 8 + ((j3 >> 4) & 7))
    perm4[...] = onehot(iota((256, 256), 1), (j2 & 15) * 16 + (j2 >> 7) * 8 + ((j2 >> 4) & 7))
    oh2[...] = onehot(iota((512, PADB), 0), slot_code)
    yb[pl.ds(3, 1)] = jnp.zeros((1, NX, 8, 16, 128), BF)
    gather(1, 1)

    def on_core(core, step, p):
        @pl.when(c == core)
        def _():
            step(p)

    on_core(0, update_products, 0)
    gather(2, 0)
    on_core(1, update_products, 1)
    gather(2, 1)
    on_core(0, update_products, 2)
    on_core(0, update_regroup, 0)
    gather(3, 0)
    gather(3, 1)
    on_core(1, update_regroup, 1)
    on_core(0, update_share, 0)
    gather(4, 0)
    stat_products(0)
    stat_products(1)
    gather(4, 1)
    on_core(1, update_share, 1)
    on_core(0, update_regroup, 2)
    stat_products(2)
    stat_products(3)
    stat_products(4)

    @pl.when(c == 0)
    def _():
        update_share(2)
        received(yb.at[1], r_y.at[1])

    @pl.when(c == 1)
    def _():
        received(yb.at[0], r_y.at[0])
        received(yb.at[2], r_x2.at[2])

    chosen = onehot(
        iota((64, 128), 1), (iota((64, 1), 0) >> 5) * 64 + 32 * c + (iota((64, 1), 0) & 31)
    )
    for i in range(8):
        lanes = mm_t(chosen, yb[:, :, i].reshape(256, 128)).astype(BF)
        wbuf[pl.ds(i * 32, 32), pl.ds(0, 256)] = lanes[:32]
        wbuf[pl.ds(i * 32, 32), pl.ds(256, 256)] = lanes[32:]
    out_u[...] = mm(wbuf[...], oh2[...]).astype(BF)[:, :NB]

    def drain_4():
        @pl.when(active)
        def _():
            sent(hsend.at[:, pl.ds(0, 15)], s_h.at[0])
            sent(gall.at[:, 0], s_own.at[0])

        @pl.when(jnp.logical_not(active))
        def _():
            sent(gall.at[:, pl.ds(0, 7)], s_ag.at[0])
            sent(gall.at[:, pl.ds(0, 7)], s_sib.at[0])

        for p in range(3):

            @pl.when(c != PAIR_CORE[p])
            def _():
                sent(bmsg.at[p], s_b.at[p])

            @pl.when(c == PAIR_CORE[p])
            def _():
                sent(bmsg.at[p, pl.ds(0, 7)], s_b.at[p])
                if p == 2:
                    sent(ub4.at[pl.ds(0, NZ - 1)], s_z2.at[p])
                    sent(gall.at[0, pl.ds(0, 7), pl.ds(0, 2)], s_x2.at[p])
                else:
                    sent(w2.at[p, pl.ds(0, NZ - 1)], s_z2.at[p])
                    sent(yb.at[p, pl.ds(0, NX - 1)], s_x2.at[p])
                    sent(yb.at[p], s_y.at[p])

    drains.append(drain_4)
    for i, (src, dst) in enumerate(((o1, out_1), (o2, out_2), (ol, out_l), (orr, out_r))):
        pltpu.make_async_copy(src, dst, s_out.at[i]).wait()
    for drain in drains:
        drain()


def onehot_lt(a, b):
    return jnp.where(a < b, 1.0, 0.0).astype(BF)


def hand_on(*refs):
    count = len(refs) // 2
    for i in range(count):
        refs[count + i][...] = refs[i][...]


def shards(grad_parts, owner_of, stats_left, stats_right, basis_left, basis_right, moment_first, moment_second):
    blocks = owner_of.shape[0]
    padded = jnp.pad(owner_of[:, 0], (0, PADB - blocks), constant_values=-1)
    anywhere = pl.BlockSpec(memory_space=pl.ANY)
    vmem = pl.BlockSpec(memory_space=pltpu.VMEM)
    rows = (SLOTS, 32, 512)
    dma = pltpu.SemaphoreType.DMA
    scratch = [
        pltpu.VMEM((1152, 256), BF),
        pltpu.VMEM((1152, 256), BF),
        pltpu.VMEM((4, NB, 512), BF),
        pltpu.VMEM((2, 2, NB, 512), BF),
        pltpu.VMEM((2, 2, NB, 512), BF),
        pltpu.VMEM((2, NB, 512), BF),
        pltpu.VMEM((PADB, 512), BF),
        pltpu.VMEM((4, 640, PADB), BF),
        pltpu.VMEM((SLOTS, 8, 16, 128), BF),
        pltpu.VMEM((SLOTS, NZ, 16, 128), BF),
        pltpu.VMEM((SLOTS, NX, 4, 16, 128), BF),
        pltpu.VMEM((SLOTS, NY, 4, 64, 128), BF),
        pltpu.VMEM((SLOTS, 512, 512), BF),
        pltpu.VMEM((SLOTS, 4, 2, 64, 512), BF),
        pltpu.VMEM((3, 4, 2, 64, 512), BF),
        pltpu.VMEM(rows, BF),
        pltpu.VMEM(rows, BF),
        pltpu.VMEM(rows, F32),
        pltpu.VMEM(rows, F32),
        pltpu.VMEM(rows, BF),
        pltpu.VMEM(rows, BF),
        pltpu.VMEM(rows, F32),
        pltpu.VMEM(rows, F32),
        pltpu.VMEM((SLOTS, 512, 256), BF),
        pltpu.VMEM((SLOTS, 16, 32, 128), BF),
        pltpu.VMEM((SLOTS, NY, 32, 128), BF),
        pltpu.VMEM((512, 512), BF),
        pltpu.VMEM((512, 512), BF),
        pltpu.VMEM((256, 256), BF),
        pltpu.VMEM((512, 512), BF),
        pltpu.VMEM((256, 256), BF),
        pltpu.VMEM((512, PADB), BF),
        pltpu.VMEM((256, 512), BF),
        pltpu.VMEM((3, NY, 32, 128), BF),
        pltpu.VMEM((3, 16, 32, 128), BF),
        pltpu.VMEM((2, 512, 128), BF),
        pltpu.VMEM((NZ, 16, 128), BF),
        pltpu.VMEM((2, NZ, 32, 128), BF),
        pltpu.VMEM((NZ, 16, 128), BF),
        pltpu.VMEM((3, NX, 8, 16, 128), BF),
        pltpu.VMEM((4, NX, 8, 16, 128), BF),
        dma((8,)),
        dma((4,)),
        dma((1,)), dma((3,)),
        dma((1,)), dma((2, 2, SUBS)), dma((SUBS,)),
        dma((1,)), dma((1,)),
        dma((1,)), dma((SLOTS,)),
        dma((1,)), dma((SLOTS,)),
        dma((1,)), dma((SLOTS,)),
        dma((1,)), dma((SLOTS,)),
        dma((1,)), dma((2, 4, 2)),
        dma((1,)), dma((2,)),
        dma((3,)), dma((3,)),
        dma((3,)), dma((3,)),
        dma((3,)), dma((3,)),
        dma((2,)), dma((2,)),
    ]
    shapes = (
        jax.ShapeDtypeStruct(rows, BF),
        jax.ShapeDtypeStruct(rows, BF),
        jax.ShapeDtypeStruct(rows, F32),
        jax.ShapeDtypeStruct(rows, F32),
        jax.ShapeDtypeStruct((256, blocks), BF),
    )
    results = pl.pallas_call(
        kernel,
        out_shape=shapes,
        in_specs=[anywhere, vmem] + [anywhere] * 6,
        out_specs=(anywhere,) * 4 + (vmem,),
        scratch_shapes=scratch,
        compiler_params=pltpu.CompilerParams(
            collective_id=0, has_side_effects=True, vmem_limit_bytes=56 * 1024 * 1024
        ),
    )(
        grad_parts[0].reshape(blocks * 8, 512),
        padded[None, :],
        stats_left[0],
        stats_right[0],
        basis_left[0],
        basis_right[0].reshape(SLOTS, 4, 2, 64, 512),
        moment_first[0],
        moment_second[0],
    )
    new_left, new_right, new_first, new_second, picked = pl.pallas_call(
        hand_on,
        out_shape=shapes,
        in_specs=[vmem] * 5,
        out_specs=(vmem,) * 5,
    )(*results)
    update = picked.reshape(8, 32, blocks).transpose(2, 0, 1)
    return (new_left[None], new_right[None], new_first[None], new_second[None], update)


def solution(mesh):
    return jax.shard_map(
        shards,
        mesh=mesh,
        in_specs=(
            P("replica", None, "owner", None),
            P(),
            P("owner", None, "replica", None),
            P("owner", None, "replica", None),
            P("owner", None, None, None),
            P("owner", None, None, None),
            P("owner", None, "replica", None),
            P("owner", None, "replica", None),
        ),
        out_specs=(
            P("owner", None, "replica", None),
            P("owner", None, "replica", None),
            P("owner", None, "replica", None),
            P("owner", None, "replica", None),
            P(None, "owner", "replica"),
        ),
        check_vma=False,
    )
```

time: 102 us -> 93.2 us (0.914)
  Pallas kernels: 100 us -> 91.2 us
    pallas_call x1, Pallas kernels: 97.8 us -> 88.9 us  [shards(): pl.pallas_call(kernel, out_shape=shapes, in_specs=[anywhere, vmem] + [any...]
where the time goes in v3:
time: 93.2 us; the launch traced here: 93 us
  Pallas kernels  91.2 us (98%)
  local copies, waits for them, and re-layouts  1.24 us (1%)
    pallas_call x1, Pallas kernels, shards(): pl.pallas_call(kernel, out_shape=shapes, in_specs=[anywhere, vmem] + [any...  88.9 us
    pallas_call x1, Pallas kernels, shards(): pl.pallas_call(hand_on, out_shape=shapes, in_specs=[vmem] * 5, out_specs=...  2.26 us

profile of v3, /device:TPU:1, one launch (start us, length us, event | category | flops | bytes accessed | tf_op | source)
XLA Modules:
  0.0 93.0 jit_solution(4986192543387485087)
XLA Ops:
  0.6 1.2 %pad.4 = s32[256]{0:T(256)} pad(s32[144]{0:T(256)} %bitcast.24, s32[]{:T(128)} %constant.0.clone.1), padding=0_112 | pad | bytes 1604 | tf_op jit(solution)/shard_map/jit(_pad)/pad | solution.py:604
  1.9 88.9 %shard_map.119 = (bf16[5,32,512]{2,1,0:T(8,128)(2,1)}, bf16[5,32,512]{2,1,0:T(8,128)(2,1)}, f32[5,32,512]{2,1,0:T(8,128)}, f32[5,32,512]{2,1,0:T(8,128)}, bf16[256,144]{1,0:T(8,128)(2,1)}) custom-call(bf16[1152,512]{1,0:T(8,128)(2,1)} %bitcast.18, s32[1,256]{1,0:T(1,128)} %bitcast.23, bf16[5,32,512]{2,1,0:T(8,128)(2,1)} %bitcast.21, ...), custom_call_target="tpu_custom_call" | custom-call | tf_op jit(solution)/shard_map/pallas_call | solution.py:674
  90.8 2.3 %shard_map.120 = (bf16[5,32,512]{2,1,0:T(8,128)(2,1)}, bf16[5,32,512]{2,1,0:T(8,128)(2,1)}, f32[5,32,512]{2,1,0:T(8,128)}, f32[5,32,512]{2,1,0:T(8,128)}, bf16[256,144]{1,0:T(8,128)(2,1)}) custom-call(bf16[5,32,512]{2,1,0:T(8,128)(2,1)} %get-tuple-element.15.refs_0_, bf16[5,32,512]{2,1,0:T(8,128)(2,1)} %get-tuple-element.16.refs_1_, ...), custom_call_target="tpu_custom_call" | custom-call | tf_op jit(solution)/shard_map/pallas_call | solution.py:693

commit v4 on v3

--- a/solution.py
+++ b/solution.py
@@ -38,7 +38,7 @@
 def kernel(
     grad, own_row, stats_l, stats_r, basis_l, basis_r, mom1, mom2,
     out_l, out_r, out_1, out_2, out_u,
-    go, gx, chunk, rs_mid, rs_end, rs_send, summed, place, v1, w1, xs1, gall,
+    owners, go, gx, chunk, rs_mid, rs_end, rs_send, summed, place, v1, w1, xs1, gall,
     ql, qr, qrs, sl, sr, m1, m2, ol, orr, o1, o2, qlt, hsend, hrecv, gf, pm, perm2, perm3, perm4, oh2, wbuf,
     bmsg, bb, ub, ub4, w2, w24, xs2, yb,
     s_in, s_out, s_core, r_core, s_rs, r_mid, r_end, s_cag, r_cag, s_z1, r_z1, s_x1, r_x1,
@@ -141,7 +141,9 @@
 
     out_of = iota((128, 1), 0)
     perm1 = onehot(iota((128, 128), 1), (out_of % 16) * 8 + out_of // 16)
-    o_row = own_row[...]
+    owners[...] = jnp.full((1, PADB), -1, jnp.int32)
+    owners[:, pl.ds(0, NB)] = own_row[...]
+    o_row = owners[...]
     e_row = onehot(iota((128, PADB), 0), o_row)
     before = mm(e_row, onehot_lt(iota((PADB, PADB), 0), iota((PADB, PADB), 1)))
     k_row = jnp.sum(before * e_row.astype(F32), axis=0, keepdims=True).astype(jnp.int32)
@@ -321,35 +323,32 @@
         hrecv[k, y] = hsend[k, rep]
         own_copy(k).start()
 
-    groups = ((0, 2), (2, 3))
-
-    def ag_part(g, t, s, d):
-        ks = pl.ds(*groups[g])
-        return gall.at[ks, t] if s < 3 else gall.at[ks, t, pl.ds(d * 2, 2)]
-
-    def ag_copy(d, s, g):
+    def ag_part(k, t, s, d):
+        return gall.at[k, t] if s < 3 else gall.at[k, t, pl.ds(d * 2, 2)]
+
+    def ag_copy(d, s, k):
         sign = 1 - 2 * d
-        ref = ag_part(g, lax.rem(y - sign * s + NY, NY), s, d)
-        return remote(ref, ref, s_ag.at[0], r_ag.at[d, s, g], at_y(y + sign, c))
-
-    def ag_arrival(d, s, g):
-        return ag_part(g, lax.rem(y - (1 - 2 * d) * (s + 1) + NY, NY), s, d)
-
-    def gather(s, g):
+        ref = ag_part(k, lax.rem(y - sign * s + NY, NY), s, d)
+        return remote(ref, ref, s_ag.at[0], r_ag.at[d, s, k], at_y(y + sign, c))
+
+    def ag_arrival(d, s, k):
+        return ag_part(k, lax.rem(y - (1 - 2 * d) * (s + 1) + NY, NY), s, d)
+
+    def gather(s, ks):
         @pl.when(jnp.logical_not(active))
         def _():
-            if s == 0:
-                for k in range(groups[g][0], sum(groups[g])):
+            for k in ks:
+                if s == 0:
                     received(gall.at[k, y], r_own.at[k])
-            for d in range(2):
+                for d in range(2):
+                    if s > 0:
+                        received(ag_arrival(d, s - 1, k), r_ag.at[d, s - 1, k])
+                    if s < 4:
+                        ag_copy(d, s, k).start()
                 if s > 0:
-                    received(ag_arrival(d, s - 1, g), r_ag.at[d, s - 1, g])
-                if s < 4:
-                    ag_copy(d, s, g).start()
-            if s > 0:
-                for d in range(2):
-                    ref = ag_arrival(d, s - 1, g)
-                    remote(ref, ref, s_sib.at[0], r_sib.at[g], sib).start()
+                    for d in range(2):
+                        ref = ag_arrival(d, s - 1, k)
+                        remote(ref, ref, s_sib.at[0], r_sib.at[k], sib).start()
 
     @pl.when(active)
     def _():
@@ -416,12 +415,9 @@
             bb[p, rep] = bmsg[p, y]
 
     def stat_products(k):
-        for g in range(2):
-            if k == groups[g][0]:
-
-                @pl.when(active)
-                def _():
-                    received(gall.at[pl.ds(*groups[g]), pl.ds(0, NY - 1)], r_sib.at[g])
+        @pl.when(active)
+        def _():
+            received(gall.at[k, pl.ds(0, NY - 1)], r_sib.at[k])
 
         for t in range(NY):
             gf[pl.ds((t // 4) * 256, 256), pl.ds((t % 4) * 128, 128)] = gall[k, t].reshape(256, 128)
@@ -429,10 +425,7 @@
         right = mm(columns, gf[...])
         orr[k] = (BETA_SECOND * sr[k].astype(F32) + (1.0 - BETA_SECOND) * right).astype(BF)
         rows = mm(pm[pl.ds(pl.multiple_of(rep * 32, 32), 32), :], gf[...]).astype(BF)
-        left = mm_t(rows, gf[...])
-        high = left.astype(BF)
-        low = (left - high.astype(F32)).astype(BF)
-        left = mm_t(high, pm[...]) + mm_t(low, pm[...])
+        left = mm_t(mm_t(rows, gf[...]).astype(BF), pm[...])
         ol[k] = (BETA_SECOND * sl[k].astype(F32) + (1.0 - BETA_SECOND) * left).astype(BF)
         for copy in out_copies(k)[2:]:
             copy.start()
@@ -492,46 +485,47 @@
         if p != 2:
             y_copy(p).start()
 
+    def on_core(core, step, p):
+        @pl.when(c == core)
+        def _():
+            step(p)
+
     slot_products(0)
-    gather(0, 0)
+    gather(0, (0, 1, 2))
     slot_products(1)
     send_back(0)
+    gather(0, (3, 4))
     slot_products(2)
-    gather(0, 1)
     slot_products(3)
     send_back(1)
-    gather(1, 0)
+    gather(1, (0, 1))
     slot_products(4)
     send_back(2)
+    gather(1, (2, 3, 4))
     j3 = iota((512, 1), 0)
     perm3[...] = onehot(iota((512, 512), 1), (j3 & 15) * 32 + (j3 >> 7) * 8 + ((j3 >> 4) & 7))
     perm4[...] = onehot(iota((256, 256), 1), (j2 & 15) * 16 + (j2 >> 7) * 8 + ((j2 >> 4) & 7))
     oh2[...] = onehot(iota((512, PADB), 0), slot_code)
     yb[pl.ds(3, 1)] = jnp.zeros((1, NX, 8, 16, 128), BF)
-    gather(1, 1)
-
-    def on_core(core, step, p):
-        @pl.when(c == core)
-        def _():
-            step(p)
-
     on_core(0, update_products, 0)
-    gather(2, 0)
+    gather(2, (0, 1))
     on_core(1, update_products, 1)
-    gather(2, 1)
+    gather(2, (2,))
     on_core(0, update_products, 2)
+    gather(2, (3, 4))
+    gather(3, (0, 1, 2))
     on_core(0, update_regroup, 0)
-    gather(3, 0)
-    gather(3, 1)
+    gather(3, (3, 4))
+    gather(4, (0, 1))
+    stat_products(0)
+    gather(4, (2,))
     on_core(1, update_regroup, 1)
+    gather(4, (3, 4))
+    stat_products(1)
     on_core(0, update_share, 0)
-    gather(4, 0)
-    stat_products(0)
-    stat_products(1)
-    gather(4, 1)
-    on_core(1, update_share, 1)
     on_core(0, update_regroup, 2)
     stat_products(2)
+    on_core(1, update_share, 1)
     stat_products(3)
     stat_products(4)
 
@@ -601,12 +595,12 @@
 
 def shards(grad_parts, owner_of, stats_left, stats_right, basis_left, basis_right, moment_first, moment_second):
     blocks = owner_of.shape[0]
-    padded = jnp.pad(owner_of[:, 0], (0, PADB - blocks), constant_values=-1)
     anywhere = pl.BlockSpec(memory_space=pl.ANY)
     vmem = pl.BlockSpec(memory_space=pltpu.VMEM)
     rows = (SLOTS, 32, 512)
     dma = pltpu.SemaphoreType.DMA
     scratch = [
+        pltpu.VMEM((1, PADB), jnp.int32),
         pltpu.VMEM((1152, 256), BF),
         pltpu.VMEM((1152, 256), BF),
         pltpu.VMEM((4, NB, 512), BF),
@@ -657,8 +651,8 @@
         dma((1,)), dma((SLOTS,)),
         dma((1,)), dma((SLOTS,)),
         dma((1,)), dma((SLOTS,)),
-        dma((1,)), dma((2, 4, 2)),
-        dma((1,)), dma((2,)),
+        dma((1,)), dma((2, 4, SLOTS)),
+        dma((1,)), dma((SLOTS,)),
         dma((3,)), dma((3,)),
         dma((3,)), dma((3,)),
         dma((3,)), dma((3,)),
@@ -682,7 +676,7 @@
         ),
     )(
         grad_parts[0].reshape(blocks * 8, 512),
-        padded[None, :],
+        owner_of.reshape(1, blocks),
         stats_left[0],
         stats_right[0],
         basis_left[0],

time: 93.2 us -> 90.3 us (0.969)
  Pallas kernels: 91.2 us -> 89.5 us
  local copies, waits for them, and re-layouts: 1.24 us -> 0 us
    pallas_call x1, Pallas kernels: 88.9 us -> 87.2 us  [shards(): pl.pallas_call(kernel, out_shape=shapes, in_specs=[anywhere, vmem] + [any...]
    pad x1 -> x0, local copies, waits for them, and re-layouts: 1.24 us -> none  [shards(): padded = jnp.pad(owner_of[:, 0], (0, PADB - blocks), constant_values=-1)]
where the time goes in v4:
time: 90.3 us; the launch traced here: 90.1 us
  Pallas kernels  89.5 us (99%)
    pallas_call x1, Pallas kernels, shards(): pl.pallas_call(kernel, out_shape=shapes, in_specs=[anywhere, vmem] + [any...  87.2 us
    pallas_call x1, Pallas kernels, shards(): pl.pallas_call(hand_on, out_shape=shapes, in_specs=[vmem] * 5, out_specs=...  2.26 us

profile of v4, /device:TPU:1, one launch (start us, length us, event | category | flops | bytes accessed | tf_op | source)
XLA Modules:
  0.0 90.1 jit_solution(13271838072282729958)
XLA Ops:
  0.6 87.2 %shard_map.119 = (bf16[5,32,512]{2,1,0:T(8,128)(2,1)}, bf16[5,32,512]{2,1,0:T(8,128)(2,1)}, f32[5,32,512]{2,1,0:T(8,128)}, f32[5,32,512]{2,1,0:T(8,128)}, bf16[256,144]{1,0:T(8,128)(2,1)}) custom-call(bf16[1152,512]{1,0:T(8,128)(2,1)} %bitcast.17, s32[1,144]{1,0:T(1,128)} %bitcast.22, bf16[5,32,512]{2,1,0:T(8,128)(2,1)} %bitcast.20, ...), custom_call_target="tpu_custom_call" | custom-call | tf_op jit(solution)/shard_map/pallas_call | solution.py:668
  87.8 2.3 %shard_map.120 = (bf16[5,32,512]{2,1,0:T(8,128)(2,1)}, bf16[5,32,512]{2,1,0:T(8,128)(2,1)}, f32[5,32,512]{2,1,0:T(8,128)}, f32[5,32,512]{2,1,0:T(8,128)}, bf16[256,144]{1,0:T(8,128)(2,1)}) custom-call(bf16[5,32,512]{2,1,0:T(8,128)(2,1)} %get-tuple-element.15.refs_0_, bf16[5,32,512]{2,1,0:T(8,128)(2,1)} %get-tuple-element.16.refs_1_, ...), custom_call_target="tpu_custom_call" | custom-call | tf_op jit(solution)/shard_map/pallas_call | solution.py:687

commit v5 on v4

--- a/solution.py
+++ b/solution.py
@@ -490,15 +490,15 @@
         def _():
             step(p)
 
+    gather(0, (0, 1, 2))
     slot_products(0)
-    gather(0, (0, 1, 2))
+    gather(0, (3, 4))
     slot_products(1)
     send_back(0)
-    gather(0, (3, 4))
     slot_products(2)
+    gather(1, (0, 1))
     slot_products(3)
     send_back(1)
-    gather(1, (0, 1))
     slot_products(4)
     send_back(2)
     gather(1, (2, 3, 4))
@@ -529,23 +529,35 @@
     stat_products(3)
     stat_products(4)
 
+    chosen = onehot(
+        iota((64, 128), 1), (iota((64, 1), 0) >> 5) * 64 + 32 * c + (iota((64, 1), 0) & 31)
+    )
+
+    def own_columns(first):
+        for i in range(8):
+            lanes = mm_t(chosen, yb[pl.ds(first, 2), :, i].reshape(128, 128)).astype(BF)
+            wbuf[pl.ds(i * 32, 32), pl.ds(first * 64, 128)] = lanes[:32]
+            wbuf[pl.ds(i * 32, 32), pl.ds(256 + first * 64, 128)] = lanes[32:]
+
+    @pl.when(c == 0)
+    def _():
+        received(yb.at[1], r_y.at[1])
+
+    @pl.when(c == 1)
+    def _():
+        received(yb.at[0], r_y.at[0])
+
+    own_columns(0)
+
     @pl.when(c == 0)
     def _():
         update_share(2)
-        received(yb.at[1], r_y.at[1])
 
     @pl.when(c == 1)
     def _():
-        received(yb.at[0], r_y.at[0])
         received(yb.at[2], r_x2.at[2])
 
-    chosen = onehot(
-        iota((64, 128), 1), (iota((64, 1), 0) >> 5) * 64 + 32 * c + (iota((64, 1), 0) & 31)
-    )
-    for i in range(8):
-        lanes = mm_t(chosen, yb[:, :, i].reshape(256, 128)).astype(BF)
-        wbuf[pl.ds(i * 32, 32), pl.ds(0, 256)] = lanes[:32]
-        wbuf[pl.ds(i * 32, 32), pl.ds(256, 256)] = lanes[32:]
+    own_columns(2)
     out_u[...] = mm(wbuf[...], oh2[...]).astype(BF)[:, :NB]
 
     def drain_4():
@@ -588,9 +600,13 @@
 
 
 def hand_on(*refs):
+    sems = refs[-1]
     count = len(refs) // 2
-    for i in range(count):
-        refs[count + i][...] = refs[i][...]
+    copies = [pltpu.make_async_copy(refs[i], refs[count + i], sems.at[i]) for i in range(count)]
+    for copy in copies:
+        copy.start()
+    for copy in copies:
+        copy.wait()
 
 
 def shards(grad_parts, owner_of, stats_left, stats_right, basis_left, basis_right, moment_first, moment_second):
@@ -688,7 +704,8 @@
         hand_on,
         out_shape=shapes,
         in_specs=[vmem] * 5,
-        out_specs=(vmem,) * 5,
+        out_specs=(anywhere,) * 5,
+        scratch_shapes=[dma((5,))],
     )(*results)
     update = picked.reshape(8, 32, blocks).transpose(2, 0, 1)
     return (new_left[None], new_right[None], new_first[None], new_second[None], update)

time: 90.3 us -> 88.7 us (0.982)
  Pallas kernels: 89.5 us -> 87.9 us
    pallas_call x1, Pallas kernels: 87.2 us -> 85.6 us  [shards(): pl.pallas_call(kernel, out_shape=shapes, in_specs=[anywhere, vmem] + [any...]
where the time goes in v5:
time: 88.7 us; the launch traced here: 88.6 us
  Pallas kernels  87.9 us (99%)
    pallas_call x1, Pallas kernels, shards(): pl.pallas_call(kernel, out_shape=shapes, in_specs=[anywhere, vmem] + [any...  85.6 us
    pallas_call x1, Pallas kernels, shards(): pl.pallas_call(hand_on, out_shape=shapes, in_specs=[vmem] * 5, out_specs=...  2.29 us

profile of v5, /device:TPU:1, one launch (start us, length us, event | category | flops | bytes accessed | tf_op | source)
XLA Modules:
  0.0 88.6 jit_solution(11421126533640241336)
XLA Ops:
  0.6 85.6 %shard_map.119 = (bf16[5,32,512]{2,1,0:T(8,128)(2,1)}, bf16[5,32,512]{2,1,0:T(8,128)(2,1)}, f32[5,32,512]{2,1,0:T(8,128)}, f32[5,32,512]{2,1,0:T(8,128)}, bf16[256,144]{1,0:T(8,128)(2,1)}) custom-call(bf16[1152,512]{1,0:T(8,128)(2,1)} %bitcast.17, s32[1,144]{1,0:T(1,128)} %bitcast.22, bf16[5,32,512]{2,1,0:T(8,128)(2,1)} %bitcast.20, ...), custom_call_target="tpu_custom_call" | custom-call | tf_op jit(solution)/shard_map/pallas_call | solution.py:684
  86.3 2.3 %shard_map.120 = (bf16[5,32,512]{2,1,0:T(8,128)(2,1)}, bf16[5,32,512]{2,1,0:T(8,128)(2,1)}, f32[5,32,512]{2,1,0:T(8,128)}, f32[5,32,512]{2,1,0:T(8,128)}, bf16[256,144]{1,0:T(8,128)(2,1)}) custom-call(bf16[5,32,512]{2,1,0:T(8,128)(2,1)} %get-tuple-element.15.refs_0_, bf16[5,32,512]{2,1,0:T(8,128)(2,1)} %get-tuple-element.16.refs_1_, ...), custom_call_target="tpu_custom_call" | custom-call | tf_op jit(solution)/shard_map/pallas_call | solution.py:703
